TPU v7x, 32 devices: a whole 2x2x4 slice. The times are simulated.
32 devices in a mesh: groups: 2 (over y), dev: 4 (over z), sub: 4 (over x, core).
Axes of the slice: x: 2, y: 2, z: 4, core: 2. Of those that a mesh axis runs over, the one named last changes fastest.
Arguments:
- embeds: float32 [4096, 1024], P(('groups', 'dev', 'sub')), parts along dimension 0
- assignment: int32 [4096], P(('groups', 'dev', 'sub')), parts along dimension 0, may hold values from 0 to 15, as said below
Outputs:
- best_match: float32 [4096], P(('groups', 'dev', 'sub')), parts along dimension 0
There are 2 independent parts, one for each index of `groups`. A program takes and returns all parts, laid end to end along the dimension named above; each array names one. Nothing has to cross between parts.
Inputs may be any that keep to these rules, and one draw needn't show every extreme that they name: `assignment`: cluster c is owned by index c // 4 of sub. Among the points of one device, at most 64 have clusters owned by one index of sub, and exactly that many in every device.
All inputs are finite; a program needn't handle non-finite values.
Results may differ from a plain program's by a relative error of at most 0.0003.
Values may be sent and summed in bfloat16 or wider, within the bound.
No kernel may reach another device: no remote copies, remote signals or barrier semaphores. Data moves between devices by JAX's collectives and lax.ppermute only.
A program may use at most 64 MiB of HBM per device.

v0:
```python
import math

import jax
import jax.numpy as jnp
from jax import lax
from jax.sharding import PartitionSpec as P

K_SUB = 4


def masked_tile(left_rows, left_ids, right_rows, right_ids):
    scores = jnp.dot(left_rows, right_rows.T, preferred_element_type=jnp.float32)
    same_group = left_ids[:, None] == right_ids[None, :]
    return (scores, same_group)


def on_device(embeds, assignment):
    row_count = embeds.shape[0]
    width = embeds.shape[1]
    owners = lax.axis_size("sub")
    capacity = row_count // 2
    slot_count = owners * capacity
    squares = jnp.sum(embeds * embeds, axis=1, keepdims=True)
    unit_rows = (embeds * lax.rsqrt(squares + 1e-06)).astype(jnp.bfloat16)
    target = assignment // K_SUB
    one_hot = (target[:, None] == jnp.arange(owners, dtype=jnp.int32)[None, :]).astype(jnp.int32)
    position = jnp.sum((jnp.cumsum(one_hot, axis=0) - one_hot) * one_hot, axis=1)
    slot_index = target * capacity + position
    send_rows = jnp.zeros((slot_count, width), jnp.bfloat16).at[slot_index].set(unit_rows)
    send_ids = jnp.full((slot_count,), -1, jnp.int32).at[slot_index].set(assignment)
    got_rows, got_ids = (
        lax.all_to_all(
            send_rows.reshape(owners, capacity, width),
            "sub",
            split_axis=0,
            concat_axis=0,
            tiled=True,
        ),
        lax.all_to_all(
            send_ids.reshape(owners, capacity), "sub", split_axis=0, concat_axis=0, tiled=True
        ),
    )
    local_rows = got_rows.reshape(slot_count, width)
    local_ids = got_ids.reshape(slot_count)
    lowest = jnp.full((slot_count,), -1.0, jnp.float32)
    my_index = lax.axis_index("dev")
    own_index = my_index * slot_count + jnp.arange(slot_count, dtype=jnp.int32)
    peer_rows = lax.all_gather(local_rows, "dev", axis=0, tiled=True)
    peer_ids = lax.all_gather(local_ids, "dev", axis=0, tiled=True)
    count = peer_rows.shape[0]
    block_rows = math.gcd(count, 512)
    stacked_rows = peer_rows.reshape(count // block_rows, block_rows, width)
    stacked_ids = peer_ids.reshape(count // block_rows, block_rows)

    def step(state, inputs):
        best, offset = state
        block_rows_here, block_ids_here = inputs
        scores, same_group = masked_tile(local_rows, local_ids, block_rows_here, block_ids_here)
        column_index = offset + jnp.arange(block_rows, dtype=jnp.int32)
        same_group = same_group & (own_index[:, None] != column_index[None, :])
        best = jnp.maximum(best, jnp.max(jnp.where(same_group, scores, jnp.float32(-1.0)), axis=1))
        return ((best, offset + block_rows), None)

    final, unused = lax.scan(step, (lowest, jnp.int32(0)), (stacked_rows, stacked_ids))
    best_slot = final[0]
    answers = lax.all_to_all(
        best_slot.reshape(owners, capacity), "sub", split_axis=0, concat_axis=0, tiled=True
    )
    return answers.reshape(slot_count)[slot_index]


def solution(mesh):
    placed = (P(("groups", "dev", "sub"), None), P(("groups", "dev", "sub")))
    return jax.shard_map(
        on_device,
        mesh=mesh,
        in_specs=placed,
        out_specs=P(("groups", "dev", "sub")),
        check_vma=False,
    )
```

profile of v0, /device:TPU:0, one launch (start us, length us, event | category | flops | bytes accessed | tf_op | source)
XLA Modules:
  0.0 92.7 jit_solution(11317117682352553930)
XLA Ops:
  6.5 0.7 and_select_fusion
  7.3 0.2 reduce_window_sum.11
  7.5 0.2 select_reduce_fusion
  7.6 0.7 compare_select_fusion
  8.3 1.2 %multiply_reduce_fusion = f32[128]{0:T(128)S(1)} fusion(f32[128,1024]{1,0:T(8,128)} %param.4), kind=kLoop, calls=%fused_computation.15 | loop fusion | flops 262016 | bytes 524800 | tf_op jit(solution)/shard_map/reduce_sum | solution.py:23
  9.5 1.9 %scatter_custom_fusion.1 = bf16[256,1024]{1,0:T(8,128)(2,1)S(1)} fusion(s32[128]{0:T(128)S(1)} %compare_select_fusion, f32[128,1024]{1,0:T(8,128)} %param.4, f32[128]{0:T(128)S(1)} %add_rsqrt_fusion, bf16[]{:T(256)} %constant.65.clone.1), kind=kCustom, calls=%fused_computation.16 | custom fusion | flops 262144 | bytes 1049090 | tf_op jit(solution)/shard_map/scatter | solution.py:29
  11.4 13.0 %all_to_all.26 = bf16[4,64,1024]{2,1,0:T(8,128)(2,1)} all-to-all(bf16[4,64,1024]{2,1,0:T(8,128)(2,1)S(1)} %bitcast.27), channel_id=1, replica_groups=mesh['groups'=2,'dev'=4,'sub'=4] {'sub'}, dimensions={0} | all-to-all | bytes 1048576 | tf_op jit(solution)/shard_map/all_to_all | solution.py:32
  24.4 1.1 %scatter_custom_fusion = s32[256]{0:T(256)S(1)} fusion(s32[128]{0:T(128)S(1)} %compare_select_fusion, s32[128]{0:T(128)} %param.5, s32[]{:T(128)} %constant.69.clone.1), kind=kCustom, calls=%fused_computation.29 | custom fusion | bytes 1536 | tf_op jit(solution)/shard_map/scatter | solution.py:30
  25.5 0.7 all_to_all.17
  26.1 3.2 %all-to-all-start = ((s32[4,1,64]{2,1,0:T(1,128)}), s32[4,1,64]{2,1,0:T(1,128)S(1)}, u32[]{:S(2)}, u32[]{:S(2)}) async-start(s32[4,1,64]{2,1,0:T(1,128)} %all_to_all.17), calls=%async_computation | async-start | bytes 4096 | tf_op jit(solution)/shard_map/all_to_all | solution.py:39
  29.3 3.7 %all-to-all-done = s32[4,1,64]{2,1,0:T(1,128)S(1)} async-done(((s32[4,1,64]{2,1,0:T(1,128)}), s32[4,1,64]{2,1,0:T(1,128)S(1)}, u32[]{:S(2)}, u32[]{:S(2)}) %all-to-all-start) | async-done | bytes 1056 | tf_op jit(solution)/shard_map/all_to_all | solution.py:39
  33.1 0.5 broadcast.51
  33.6 0.6 reduce.7
  34.3 11.8 %all-gather = s32[4,1,256]{2,1,0:T(1,128)S(1)} all-gather(s32[1,1,256]{2,1,0:T(1,128)S(1)} %reshape.74), channel_id=1, replica_groups=mesh['groups'=2,'dev'=4,'sub'=4] {'dev'}, dimensions={0}, use_global_device_ids=true | all-gather | bytes 5120 | tf_op jit(solution)/shard_map/all_gather | solution.py:49
  46.1 25.2 %all-gather.3.cloned.1.call-done = bf16[1024,1024]{1,0:T(8,128)(2,1)} async-done(((bf16[256,1024]{1,0:T(8,128)(2,1)}), bf16[1024,1024]{1,0:T(8,128)(2,1)}) %all-gather.3.cloned.1.call-update) | async-done | bytes 2097168 | tf_op jit(solution)/shard_map/all_gather | solution.py:48
  71.3 3.9 %while.15 = (s32[]{:T(128)}, f32[256]{0:T(256)S(1)}, s32[4,64]{1,0:T(4,128)}, s32[2,512]{1,0:T(2,128)S(1)}, bf16[2,512,1024]{2,1,0:T(8,128)(2,1)}, /*index=5*/bf...) while((s32[]{:T(128)}, f32[256]{0:T(256)S(1)}, ...), condition=%wide.wide.region_7.8_spmd.clone, body=%wide.wide.region_5.7_spmd.clone.sunk | while | flops 269091840 | bytes 1590927 | solution.py:64
  71.3 1.9 %fusion.22 = f32[256]{0:T(256)S(1)} fusion(bf16[256,1024]{1,0:T(8,128)(2,1)} %get-tuple-element.275, bf16[2,512,1024]{2,1,0:T(8,128)(2,1)} %get-tuple-element.274, s32[]{:T(128)} %get-tuple-element.259, s32[256]{0:T(256)S(1)} %iota_add_fusion.6, s32[256]{0:T(256)S(1)} %get-tuple-element.277, s32[512]{0:T(512)S(1)} %iota_add_fusion.7, ...), kind=kOutput, calls=%fused_computation.6.clone.clone.1 | convolution fusion | flops 269090560 | bytes 1580544 | tf_op jit(solution)/shard_map/while/body/eval_jaxpr/dot_general | solution.py:12
  73.2 1.9 %fusion.22 = f32[256]{0:T(256)S(1)} fusion(bf16[256,1024]{1,0:T(8,128)(2,1)} %get-tuple-element.275, bf16[2,512,1024]{2,1,0:T(8,128)(2,1)} %get-tuple-element.274, s32[]{:T(128)} %get-tuple-element.259, s32[256]{0:T(256)S(1)} %iota_add_fusion.6, s32[256]{0:T(256)S(1)} %get-tuple-element.277, s32[512]{0:T(512)S(1)} %iota_add_fusion.7, ...), kind=kOutput, calls=%fused_computation.6.clone.clone.1 | convolution fusion | flops 269090560 | bytes 1580544 | tf_op jit(solution)/shard_map/while/body/eval_jaxpr/dot_general | solution.py:12
  75.1 0.7 all_to_all.21
  75.8 3.2 %all-to-all-start.2 = ((f32[4,1,64]{2,1,0:T(1,128)}), f32[4,1,64]{2,1,0:T(1,128)S(1)}, u32[]{:S(2)}, u32[]{:S(2)}) async-start(f32[4,1,64]{2,1,0:T(1,128)} %all_to_all.21), calls=%async_computation.2 | async-start | bytes 4096 | tf_op jit(solution)/shard_map/all_to_all | solution.py:66
  79.1 3.7 %all-to-all-done.2 = f32[4,1,64]{2,1,0:T(1,128)S(1)} async-done(((f32[4,1,64]{2,1,0:T(1,128)}), f32[4,1,64]{2,1,0:T(1,128)S(1)}, u32[]{:S(2)}, u32[]{:S(2)}) %all-to-all-start.2) | async-done | bytes 1056 | tf_op jit(solution)/shard_map/all_to_all | solution.py:66
  82.8 0.5 broadcast.52
  83.3 0.7 reduce.8
  84.0 1.8 %gather_fusion = f32[128]{0:T(128)} fusion(f32[256]{0:T(256)S(1)} %reshape.46, s32[1024]{0:T(1024)S(1)} %pad_clamp_fusion), kind=kCustom, calls=%fused_computation | custom fusion | bytes 1536 | tf_op jit(solution)/shard_map/gather | solution.py:69
  (21 shorter events, 0.5 us)
Async XLA Ops:
  6.5 64.7 %all-gather.3.cloned.1.call-start = ((), (), s32[]{:S(2)}) async-start(), calls=%async_computation.3 | async-start | bytes 2621440 | tf_op jit(solution)/shard_map/all_gather | solution.py:48
  26.1 6.9 %all-to-all-start = ((s32[4,1,64]{2,1,0:T(1,128)}), s32[4,1,64]{2,1,0:T(1,128)S(1)}, u32[]{:S(2)}, u32[]{:S(2)}) async-start(s32[4,1,64]{2,1,0:T(1,128)} %all_to_all.17), calls=%async_computation | async-start | bytes 4096 | tf_op jit(solution)/shard_map/all_to_all | solution.py:39
  33.0 38.2 %copy-start = (s32[4,1,64]{2,1,0:T(1,128)}, s32[4,1,64]{2,1,0:T(1,128)S(1)}, u32[]{:S(2)}) copy-start(s32[4,1,64]{2,1,0:T(1,128)S(1)} %all-to-all-done) | copy-start | bytes 3076
  75.8 7.0 %all-to-all-start.2 = ((f32[4,1,64]{2,1,0:T(1,128)}), f32[4,1,64]{2,1,0:T(1,128)S(1)}, u32[]{:S(2)}, u32[]{:S(2)}) async-start(f32[4,1,64]{2,1,0:T(1,128)} %all_to_all.21), calls=%async_computation.2 | async-start | bytes 4096 | tf_op jit(solution)/shard_map/all_to_all | solution.py:66
Sparse Core Ops, SparseCore 0:
  24.5 46.7 all-gather.2
where the time goes:
time: 93.1 us; the launch traced here: 92.7 us
  waiting for transfers between devices  32.6 us (35%)
  blocking collectives  24.7 us (27%)
  between operations  13.5 us (15%)
  starting transfers between devices  6.42 us (7%)
  other arithmetic  6.13 us (7%)
  local copies, waits for them, and re-layouts  5.5 us (6%)
  matrix products  3.71 us (4%)
    all_gather x1, waiting for transfers between devices, on_device(): peer_rows = lax.all_gather(local_rows, 'dev', axis=0, tiled=True)  25.2 us
    all_to_all x1, blocking collectives, on_device(): lax.all_to_all(send_rows.reshape(owners, capacity, width), 'sub', split_a...  13 us
    all_gather x1, blocking collectives, on_device(): peer_ids = lax.all_gather(local_ids, 'dev', axis=0, tiled=True)  11.8 us
    dot_general x2, matrix products, masked_tile(): jnp.dot(left_rows, right_rows.T, preferred_element_type=jnp.float32)  3.71 us
    all_to_all x1, waiting for transfers between devices, on_device(): lax.all_to_all(best_slot.reshape(owners, capacity), 'sub', split_axis=0,...  3.7 us
    all_to_all x1, waiting for transfers between devices, on_device(): lax.all_to_all(send_ids.reshape(owners, capacity), 'sub', split_axis=0, c...  3.69 us
    all_to_all x1, starting transfers between devices, on_device(): lax.all_to_all(best_slot.reshape(owners, capacity), 'sub', split_axis=0,...  3.24 us
    all_to_all x1, starting transfers between devices, on_device(): lax.all_to_all(send_ids.reshape(owners, capacity), 'sub', split_axis=0, c...  3.17 us
  transfers between devices with their start and end apart: 3, of which 3 were waited for; matrix products, arithmetic and copies ran while one was open for 3% of the time, Pallas kernels for 0%

commit v1 on v0

v1 whole, which is shorter than its diff:
```python
import functools

import jax
import jax.numpy as jnp
from jax import lax
from jax.experimental import pallas as pl
from jax.experimental.pallas import tpu as pltpu
from jax.sharding import PartitionSpec as P

LANES = 128
ID_ROWS = 16
LOWEST = -1.0


def pack_kernel(embeds_ref, ids_ref, out_ref):
    rows, width = embeds_ref.shape
    embeds = embeds_ref[...]
    squares = jnp.sum(embeds * embeds, axis=1, keepdims=True)
    unit = (embeds * lax.rsqrt(squares + 1e-06)).astype(jnp.bfloat16)
    for block in range(width // LANES):
        out_ref[pl.ds(block * rows, rows), :] = unit[:, block * LANES : (block + 1) * LANES]
    ids = ids_ref[...].astype(jnp.float32)
    out_ref[pl.ds(width // LANES * rows, ID_ROWS), :] = jnp.broadcast_to(
        ids, (ID_ROWS, rows)
    ).astype(jnp.bfloat16)


def load_rows(ref, rows):
    blocks = (ref.shape[0] - ID_ROWS) // rows
    return jnp.concatenate([ref[pl.ds(b * rows, rows), :] for b in range(blocks)], axis=1)


def load_ids(ref, rows):
    start = ref.shape[0] - ID_ROWS
    return ref[pl.ds(start, ID_ROWS), :].astype(jnp.float32)[:1, :]


def row_maxima(masked):
    best = functools.reduce(jnp.maximum, masked)
    return jnp.max(best.T, axis=0, keepdims=True)


def score_kernel(*refs, rows, own, want_rows, want_columns):
    outs = int(want_rows) + int(want_columns)
    left_ref, column_refs, out_refs = refs[0], refs[1 : len(refs) - outs], refs[len(refs) - outs :]
    left = load_rows(left_ref, rows)
    left_ids = jnp.broadcast_to(load_ids(left_ref, rows), (rows, rows)).T
    masked = []
    for k, ref in enumerate(column_refs):
        scores = lax.dot_general(
            left,
            load_rows(ref, rows),
            (((1,), (1,)), ((), ())),
            preferred_element_type=jnp.float32,
        )
        same = left_ids == load_ids(ref, rows)
        if own and k == 0:
            down = lax.broadcasted_iota(jnp.int32, (rows, rows), 0)
            across = lax.broadcasted_iota(jnp.int32, (rows, rows), 1)
            same = same & (down != across)
        masked.append(jnp.where(same, scores, jnp.float32(LOWEST)))
    if want_rows:
        out_refs[0][...] = row_maxima(masked)
    if want_columns:
        for k, block in enumerate(masked):
            out_refs[-1][pl.ds(k, 1), :] = jnp.max(block, axis=0, keepdims=True)


def scores(left, column, rows, own=False, want_rows=True, want_columns=True):
    width = (left.shape[0] - ID_ROWS) // rows * LANES
    shapes = [(1, rows)] * want_rows + [(len(column), rows)] * want_columns
    return pl.pallas_call(
        functools.partial(
            score_kernel, rows=rows, own=own, want_rows=want_rows, want_columns=want_columns
        ),
        out_shape=[jax.ShapeDtypeStruct(shape, jnp.float32) for shape in shapes],
        cost_estimate=pl.CostEstimate(
            flops=2 * rows * rows * len(column) * width,
            bytes_accessed=2 * left.size * (1 + len(column)),
            transcendentals=0,
        ),
        compiler_params=pltpu.CompilerParams(vmem_limit_bytes=32 * 1024 * 1024),
    )(left, *column)


def pack(embeds, ids):
    rows, width = embeds.shape
    return pl.pallas_call(
        pack_kernel,
        out_shape=jax.ShapeDtypeStruct((width // LANES * rows + ID_ROWS, LANES), jnp.bfloat16),
        compiler_params=pltpu.CompilerParams(vmem_limit_bytes=32 * 1024 * 1024),
    )(embeds, ids.reshape(1, rows))


def column_order(count):
    return [0, 3, 1, 2] if count == 4 else list(range(count))


def on_device(embeds, assignment):
    rows = embeds.shape[0]
    columns, lanes = lax.axis_size("dev"), lax.axis_size("sub")
    order = column_order(columns)

    def along_dev(value, step):
        pairs = [(order[i], order[(i + step) % columns]) for i in range(columns)]
        return lax.ppermute(value, "dev", pairs)

    def along_sub(value, flip):
        return lax.ppermute(value, "sub", [(i, i ^ flip) for i in range(lanes)])

    own = pack(embeds, assignment)
    turns = list(range(1, (columns + 1) // 2))
    moved = {step: along_dev(own, step) for step in turns}
    swap = columns // 2 if columns % 2 == 0 else 0
    if swap:
        swapped = along_dev(own, swap)
    column = {0: own}
    for flip in range(2, lanes, 2):
        column[flip] = along_sub(own, flip)
    for flip in range(0, lanes, 2):
        column[flip + 1] = along_sub(column[flip], 1)
    column = [column[k] for k in range(lanes)]

    best = [scores(own, column, rows, own=True, want_columns=False)[0]]
    partial = []
    if swap:
        partial.append(scores(swapped, column, rows, want_rows=False)[0])
    for step in turns:
        row_best, column_best = scores(moved[step], column, rows)
        best.append(along_dev(row_best, -step))
        partial.append(column_best)
    total = functools.reduce(jnp.maximum, partial)
    pair = total[:2]
    for flip in range(2, lanes, 2):
        pair = jnp.maximum(pair, along_sub(total[flip : flip + 2], flip))
    best.append(pair[:1])
    best.append(along_sub(pair[1:], 1))
    return functools.reduce(jnp.maximum, best).reshape(rows)


def solution(mesh):
    placed = (P(("groups", "dev", "sub"), None), P(("groups", "dev", "sub")))
    return jax.shard_map(
        on_device,
        mesh=mesh,
        in_specs=placed,
        out_specs=P(("groups", "dev", "sub")),
        check_vma=False,
    )
```

time: 93.1 us -> 35 us (0.38)
  blocking collectives: 24.7 us -> 0 us
  between operations: 13.5 us -> 0.06 us
  waiting for transfers between devices: 32.6 us -> 19.2 us
  other arithmetic: 6.13 us -> 0.52 us
  starting transfers between devices: 6.42 us -> 11.7 us
  local copies, waits for them, and re-layouts: 5.5 us -> 1.71 us
  matrix products: 3.71 us -> 0 us
  Pallas kernels: 0 us -> 1.6 us
    all_gather x1 -> x0, waiting for transfers between devices: 25.2 us -> none  [on_device(): peer_rows = lax.all_gather(local_rows, 'dev', axis=0, tiled=True)]
    ppermute x0 -> x8, waiting for transfers between devices: none -> 19.2 us  [the longest x3 14.1 us: along_dev(): return lax.ppermute(value, 'dev', pairs)]
    all_to_all x1 -> x0, blocking collectives: 13 us -> none  [on_device(): lax.all_to_all(send_rows.reshape(owners, capacity, width), 'sub', split_a...]
    all_gather x1 -> x0, blocking collectives: 11.8 us -> none  [on_device(): peer_ids = lax.all_gather(local_ids, 'dev', axis=0, tiled=True)]
    ppermute x0 -> x8, starting transfers between devices: none -> 11.7 us  [the longest x3 7.12 us: along_dev(): return lax.ppermute(value, 'dev', pairs)]
    all_to_all x2 -> x0, waiting for transfers between devices: 7.4 us -> none  [the longest x1 3.7 us: on_device(): lax.all_to_all(best_slot.reshape(owners, capacity), 'sub', split_axis=0,...]
    all_to_all x2 -> x0, starting transfers between devices: 6.42 us -> none  [the longest x1 3.24 us: on_device(): lax.all_to_all(best_slot.reshape(owners, capacity), 'sub', split_axis=0,...]
    dot_general x2 -> x0, matrix products: 3.71 us -> none  [masked_tile(): jnp.dot(left_rows, right_rows.T, preferred_element_type=jnp.float32)]
  transfers between devices with their start and end apart: 3 -> 8, of which waited for: 3 -> 4; matrix products, arithmetic and copies ran while one was open for 3% -> 0% of each run, Pallas kernels for 0% -> 3%
where the time goes in v1:
time: 35 us; the launch traced here: 34.8 us
  waiting for transfers between devices  19.2 us (55%)
  starting transfers between devices  11.7 us (33%)
  local copies, waits for them, and re-layouts  1.71 us (5%)
  Pallas kernels  1.6 us (5%)
  other arithmetic  0.52 us (1%)
    ppermute x3, waiting for transfers between devices, along_dev(): return lax.ppermute(value, 'dev', pairs)  14.1 us
    ppermute x3, starting transfers between devices, along_dev(): return lax.ppermute(value, 'dev', pairs)  7.12 us
    ppermute x5, waiting for transfers between devices, along_sub(): return lax.ppermute(value, 'sub', [(i, i ^ flip) for i in range(lanes)])  5.16 us
    ppermute x5, starting transfers between devices, along_sub(): return lax.ppermute(value, 'sub', [(i, i ^ flip) for i in range(lanes)])  4.62 us
    unnamed x4, local copies, waits for them, and re-layouts  1.7 us
    pallas_call x3, Pallas kernels, scores(): pl.pallas_call(functools.partial(score_kernel, rows=rows, own=own, want_r...  1.47 us
  transfers between devices with their start and end apart: 8, of which 4 were waited for; matrix products, arithmetic and copies ran while one was open for 0% of the time, Pallas kernels for 3%

profile of v1, /device:TPU:0, one launch (start us, length us, event | category | flops | bytes accessed | tf_op | source)
XLA Modules:
  0.0 34.8 jit_solution(14106397703827163094)
XLA Ops:
  0.0 0.0 copy-start.1
  0.0 0.7 %copy-done.1 = s32[128]{0:T(128)S(1)} copy-done((s32[128]{0:T(128)S(1)}, s32[128]{0:T(128)}, u32[]{:S(2)}) %copy-start.1) | copy-done | bytes 536
  0.7 1.0 %copy-done = f32[128,1024]{1,0:T(8,128)S(1)} copy-done((f32[128,1024]{1,0:T(8,128)S(1)}, f32[128,1024]{1,0:T(8,128)}, u32[]{:S(2)}) %copy-start) | copy-done | bytes 524312
  1.7 0.1 shard_map.28.refs_0_.refs_1_
  1.8 3.0 %collective-permute-start.1 = (bf16[1040,128]{1,0:T(8,128)(2,1)S(1)}, bf16[1040,128]{1,0:T(8,128)(2,1)S(1)}, u32[]{:S(2)}, u32[]{:S(2)}) collective-permute-start(bf16[1040,128]{1,0:T(8,128)(2,1)S(1)} %shard_map.28.refs_0_.refs_1_), channel_id=1, source_target_pairs={{0,2},{1,3},{2,0},{3,1},{4,6},{5,7},{6,4},{7,5},{8,10},{9,11},{10,... | collective-permute-start | bytes 798728 | tf_op jit(solution)/shard_map/ppermute | solution.py:109
  4.8 1.6 %collective-permute-start.5 = (bf16[1040,128]{1,0:T(8,128)(2,1)S(1)}, bf16[1040,128]{1,0:T(8,128)(2,1)S(1)}, u32[]{:S(2)}, u32[]{:S(2)}) collective-permute-start(bf16[1040,128]{1,0:T(8,128)(2,1)S(1)} %shard_map.28.refs_0_.refs_1_), channel_id=1, source_target_pairs={{0,4},{12,8},{4,0},{8,12},{1,5},{13,9},{5,1},{9,13},{2,6},{14,10},... | collective-permute-start | bytes 798728 | tf_op jit(solution)/shard_map/ppermute | solution.py:106
  6.4 0.0 collective-permute-start
  6.4 4.8 %collective-permute-done.1.refs_3_ = bf16[1040,128]{1,0:T(8,128)(2,1)S(1)} collective-permute-done((bf16[1040,128]{1,0:T(8,128)(2,1)S(1)}, bf16[1040,128]{1,0:T(8,128)(2,1)S(1)}, u32[]{:S(2)}, u32[]{:S(2)}) %collective-permute-start.1) | collective-permute-done | bytes 266272 | tf_op jit(solution)/shard_map/ppermute | solution.py:109
  11.2 0.0 collective-permute-start.2
  11.2 3.9 %collective-permute-start.3 = (bf16[1040,128]{1,0:T(8,128)(2,1)S(1)}, bf16[1040,128]{1,0:T(8,128)(2,1)S(1)}, u32[]{:S(2)}, u32[]{:S(2)}) collective-permute-start(bf16[1040,128]{1,0:T(8,128)(2,1)S(1)} %shard_map.28.refs_0_.refs_1_), channel_id=1, source_target_pairs={{0,12},{12,4},{4,8},{8,0},{1,13},{13,5},{5,9},{9,1},{2,14},{14,6},... | collective-permute-start | bytes 798728 | tf_op jit(solution)/shard_map/ppermute | solution.py:106
  15.1 0.0 collective-permute-done.5.refs_0_
  15.1 0.0 collective-permute-done.refs_2_
  15.1 0.0 collective-permute-done.2.refs_4_
  15.1 0.4 %shard_map.31 = f32[4,128]{1,0:T(4,128)S(1)} custom-call(bf16[1040,128]{1,0:T(8,128)(2,1)S(1)} %collective-permute-done.5.refs_0_, bf16[1040,128]{1,0:T(8,128)(2,1)S(1)} %shard_map.28.refs_0_.refs_1_, bf16[1040,128]{1,0:T(8,128)(2,1)S(1)} %collective-permute-done.refs_2_, bf16[1040,128]{1,0:T(8,128)(2,1)S(1)} %collective-permute-done.1.refs_3_, ...), custom_call_target="tpu_custom_call" | custom-call | flops 134217728 | bytes 1331200 | tf_op jit(solution)/shard_map/pallas_call | solution.py:72
  15.6 11.3 %collective-permute-done.3.refs_0_ = bf16[1040,128]{1,0:T(8,128)(2,1)S(1)} collective-permute-done((bf16[1040,128]{1,0:T(8,128)(2,1)S(1)}, bf16[1040,128]{1,0:T(8,128)(2,1)S(1)}, u32[]{:S(2)}, u32[]{:S(2)}) %collective-permute-start.3) | collective-permute-done | bytes 266272 | tf_op jit(solution)/shard_map/ppermute | solution.py:106
  26.8 0.5 %shard_map.30 = (f32[1,128]{1,0:T(1,128)S(1)}, f32[4,128]{1,0:T(4,128)S(1)}) custom-call(bf16[1040,128]{1,0:T(8,128)(2,1)S(1)} %collective-permute-done.3.refs_0_, bf16[1040,128]{1,0:T(8,128)(2,1)S(1)} %shard_map.28.refs_0_.refs_1_, bf16[1040,128]{1,0:T(8,128)(2,1)S(1)} %collective-permute-done.refs_2_, ...), custom_call_target="tpu_custom_call" | custom-call | flops 134217728 | bytes 1331200 | tf_op jit(solution)/shard_map/pallas_call | solution.py:72
  27.4 1.6 %collective-permute-start.6 = (f32[2,128]{1,0:T(2,128)S(1)}, f32[2,128]{1,0:T(2,128)S(1)}, u32[]{:S(2)}, u32[]{:S(2)}) collective-permute-start(f32[2,128]{1,0:T(2,128)S(1)} %slice.13), channel_id=1, source_target_pairs={{0,2},{1,3},{2,0},{3,1},{4,6},{5,7},{6,4},{7,5},{8,10},{9,11},{10,... | collective-permute-start | bytes 3080 | tf_op jit(solution)/shard_map/ppermute | solution.py:109
  29.0 1.7 %collective-permute-start.4 = (f32[1,128]{1,0:T(1,128)S(1)}, f32[1,128]{1,0:T(1,128)S(1)}, u32[]{:S(2)}, u32[]{:S(2)}) collective-permute-start(f32[1,128]{1,0:T(1,128)S(1)} %get-tuple-element.7), channel_id=1, source_target_pairs={{0,8},{12,0},{4,12},{8,4},{1,9},{13,1},{5,13},{9,5},{2,10},{14,2},... | collective-permute-start | bytes 1544 | tf_op jit(solution)/shard_map/ppermute | solution.py:106
  30.7 0.3 collective-permute-done.6
  31.0 0.0 collective-permute-start.7
  31.0 0.5 %shard_map.29 = f32[1,128]{1,0:T(1,128)S(1)} custom-call(bf16[1040,128]{1,0:T(8,128)(2,1)S(1)} %shard_map.28.refs_0_.refs_1_, bf16[1040,128]{1,0:T(8,128)(2,1)S(1)} %shard_map.28.refs_0_.refs_1_, bf16[1040,128]{1,0:T(8,128)(2,1)S(1)} %collective-permute-done.refs_2_, bf16[1040,128]{1,0:T(8,128)(2,1)S(1)} %collective-permute-done.1.refs_3_, ...), custom_call_target="tpu_custom_call" | custom-call | flops 134217728 | bytes 1331200 | tf_op jit(solution)/shard_map/pallas_call | solution.py:72
  31.6 2.8 %collective-permute-done.4 = f32[1,128]{1,0:T(1,128)S(1)} collective-permute-done((f32[1,128]{1,0:T(1,128)S(1)}, f32[1,128]{1,0:T(1,128)S(1)}, u32[]{:S(2)}, u32[]{:S(2)}) %collective-permute-start.4) | collective-permute-done | bytes 544 | tf_op jit(solution)/shard_map/ppermute | solution.py:106
  34.3 0.0 collective-permute-done.7
  34.3 0.5 %maximum_bitcast_fusion = f32[128]{0:T(128)} fusion(f32[1,128]{1,0:T(1,128)S(1)} %collective-permute-done.7, f32[2,128]{1,0:T(2,128)S(1)} %slice_maximum_fusion, f32[1,128]{1,0:T(1,128)S(1)} %shard_map.29, f32[1,128]{1,0:T(1,128)S(1)} %collective-permute-done.4), kind=kLoop, calls=%fused_computation.1 | loop fusion | flops 384 | bytes 2560 | tf_op jit(solution)/shard_map/reshape | solution.py:138
  (5 shorter events, 0.0 us)
Async XLA Ops:
  0.0 0.7 %copy-start.1 = (s32[128]{0:T(128)S(1)}, s32[128]{0:T(128)}, u32[]{:S(2)}) copy-start(s32[128]{0:T(128)} %param.3) | copy-start | bytes 1540
  0.7 1.0 %copy-start = (f32[128,1024]{1,0:T(8,128)S(1)}, f32[128,1024]{1,0:T(8,128)}, u32[]{:S(2)}) copy-start(f32[128,1024]{1,0:T(8,128)} %embeds_ref.1) | copy-start | bytes 1572868
  1.8 9.4 %collective-permute-start.1 = (bf16[1040,128]{1,0:T(8,128)(2,1)S(1)}, bf16[1040,128]{1,0:T(8,128)(2,1)S(1)}, u32[]{:S(2)}, u32[]{:S(2)}) collective-permute-start(bf16[1040,128]{1,0:T(8,128)(2,1)S(1)} %shard_map.28.refs_0_.refs_1_), channel_id=1, source_target_pairs={{0,2},{1,3},{2,0},{3,1},{4,6},{5,7},{6,4},{7,5},{8,10},{9,11},{10,... | collective-permute-start | bytes 798728 | tf_op jit(solution)/shard_map/ppermute | solution.py:109
  4.8 10.3 %collective-permute-start.5 = (bf16[1040,128]{1,0:T(8,128)(2,1)S(1)}, bf16[1040,128]{1,0:T(8,128)(2,1)S(1)}, u32[]{:S(2)}, u32[]{:S(2)}) collective-permute-start(bf16[1040,128]{1,0:T(8,128)(2,1)S(1)} %shard_map.28.refs_0_.refs_1_), channel_id=1, source_target_pairs={{0,4},{12,8},{4,0},{8,12},{1,5},{13,9},{5,1},{9,13},{2,6},{14,10},... | collective-permute-start | bytes 798728 | tf_op jit(solution)/shard_map/ppermute | solution.py:106
  6.4 8.7 %collective-permute-start = (bf16[1040,128]{1,0:T(8,128)(2,1)S(1)}, bf16[1040,128]{1,0:T(8,128)(2,1)S(1)}, u32[]{:S(2)}, u32[]{:S(2)}) collective-permute-start(bf16[1040,128]{1,0:T(8,128)(2,1)S(1)} %shard_map.28.refs_0_.refs_1_), channel_id=1, source_target_pairs={{0,1},{1,0},{2,3},{3,2},{4,5},{5,4},{6,7},{7,6},{8,9},{9,8},{10,11... | collective-permute-start | bytes 798728 | tf_op jit(solution)/shard_map/ppermute | solution.py:109
  11.2 3.9 %collective-permute-start.2 = (bf16[1040,128]{1,0:T(8,128)(2,1)S(1)}, bf16[1040,128]{1,0:T(8,128)(2,1)S(1)}, u32[]{:S(2)}, u32[]{:S(2)}) collective-permute-start(bf16[1040,128]{1,0:T(8,128)(2,1)S(1)} %collective-permute-done.1.refs_3_), channel_id=1, source_target_pairs={{0,1},{1,0},{2,3},{3,2},{4,5},{5,4},{6,7},{7,6},{8,9},{9,8},{10,11... | collective-permute-start | bytes 798728 | tf_op jit(solution)/shard_map/ppermute | solution.py:109
  11.2 15.6 %collective-permute-start.3 = (bf16[1040,128]{1,0:T(8,128)(2,1)S(1)}, bf16[1040,128]{1,0:T(8,128)(2,1)S(1)}, u32[]{:S(2)}, u32[]{:S(2)}) collective-permute-start(bf16[1040,128]{1,0:T(8,128)(2,1)S(1)} %shard_map.28.refs_0_.refs_1_), channel_id=1, source_target_pairs={{0,12},{12,4},{4,8},{8,0},{1,13},{13,5},{5,9},{9,1},{2,14},{14,6},... | collective-permute-start | bytes 798728 | tf_op jit(solution)/shard_map/ppermute | solution.py:106
  27.4 3.6 %collective-permute-start.6 = (f32[2,128]{1,0:T(2,128)S(1)}, f32[2,128]{1,0:T(2,128)S(1)}, u32[]{:S(2)}, u32[]{:S(2)}) collective-permute-start(f32[2,128]{1,0:T(2,128)S(1)} %slice.13), channel_id=1, source_target_pairs={{0,2},{1,3},{2,0},{3,1},{4,6},{5,7},{6,4},{7,5},{8,10},{9,11},{10,... | collective-permute-start | bytes 3080 | tf_op jit(solution)/shard_map/ppermute | solution.py:109
  29.0 5.3 %collective-permute-start.4 = (f32[1,128]{1,0:T(1,128)S(1)}, f32[1,128]{1,0:T(1,128)S(1)}, u32[]{:S(2)}, u32[]{:S(2)}) collective-permute-start(f32[1,128]{1,0:T(1,128)S(1)} %get-tuple-element.7), channel_id=1, source_target_pairs={{0,8},{12,0},{4,12},{8,4},{1,9},{13,1},{5,13},{9,5},{2,10},{14,2},... | collective-permute-start | bytes 1544 | tf_op jit(solution)/shard_map/ppermute | solution.py:106
  31.0 3.3 %collective-permute-start.7 = (f32[1,128]{1,0:T(1,128)S(1)}, f32[1,128]{1,0:T(1,128)S(1)}, u32[]{:S(2)}, u32[]{:S(2)}) collective-permute-start(f32[1,128]{1,0:T(1,128)S(1)} %slice.15), channel_id=1, source_target_pairs={{0,1},{1,0},{2,3},{3,2},{4,5},{5,4},{6,7},{7,6},{8,9},{9,8},{10,11... | collective-permute-start | bytes 1544 | tf_op jit(solution)/shard_map/ppermute | solution.py:109

commit v2 on v1

v2 whole, which is shorter than its diff:
```python
import functools

import jax
import jax.numpy as jnp
from jax import lax
from jax.experimental import pallas as pl
from jax.experimental.pallas import tpu as pltpu
from jax.sharding import PartitionSpec as P

LANES = 128
ID_ROWS = 16
LOWEST = -1.0
VMEM_BYTES = 16 * 1024 * 1024


def pack_kernel(embeds_ref, out_ref):
    rows, width = embeds_ref.shape
    embeds = embeds_ref[...]
    squares = jnp.sum(embeds * embeds, axis=1, keepdims=True)
    unit = (embeds * lax.rsqrt(squares + 1e-06)).astype(jnp.bfloat16)
    for block in range(width // LANES):
        out_ref[pl.ds(block * rows, rows), :] = unit[:, block * LANES : (block + 1) * LANES]


def label_kernel(packed_ref, ids_ref, out_ref):
    del packed_ref
    start = out_ref.shape[0] - ID_ROWS
    ids = jnp.broadcast_to(ids_ref[...].astype(jnp.float32), (ID_ROWS, ids_ref.shape[1]))
    out_ref[pl.ds(start, ID_ROWS), :] = ids.astype(jnp.bfloat16)


def pack(embeds, ids):
    rows, width = embeds.shape
    cells = width // LANES * rows
    shape = jax.ShapeDtypeStruct((cells + ID_ROWS, LANES), jnp.bfloat16)
    packed = pl.pallas_call(
        pack_kernel,
        out_shape=shape,
        compiler_params=pltpu.CompilerParams(vmem_limit_bytes=VMEM_BYTES),
    )(embeds)
    return pl.pallas_call(
        label_kernel,
        out_shape=shape,
        input_output_aliases={0: 0},
        compiler_params=pltpu.CompilerParams(vmem_limit_bytes=VMEM_BYTES),
    )(packed, ids.reshape(1, rows))


def load_rows(ref, rows):
    blocks = (ref.shape[0] - ID_ROWS) // rows
    return jnp.concatenate([ref[pl.ds(b * rows, rows), :] for b in range(blocks)], axis=1)


def load_ids(ref):
    start = ref.shape[0] - ID_ROWS
    return ref[pl.ds(start, ID_ROWS), :].astype(jnp.float32)[:1, :]


def masked_scores(left_refs, column_refs, rows, own):
    left = jnp.concatenate([load_rows(ref, rows) for ref in left_refs], axis=0)
    left_ids = [jnp.broadcast_to(load_ids(ref), (rows, rows)).T for ref in left_refs]
    masked = [[] for _ in left_refs]
    for k, ref in enumerate(column_refs):
        scores = lax.dot_general(
            left,
            load_rows(ref, rows),
            (((1,), (1,)), ((), ())),
            preferred_element_type=jnp.float32,
        )
        ids = load_ids(ref)
        for t in range(len(left_refs)):
            same = left_ids[t] == ids
            if own and k == 0:
                down = lax.broadcasted_iota(jnp.int32, (rows, rows), 0)
                across = lax.broadcasted_iota(jnp.int32, (rows, rows), 1)
                same = same & (down != across)
            part = scores[t * rows : (t + 1) * rows, :]
            masked[t].append(jnp.where(same, part, jnp.float32(LOWEST)))
    return masked


def row_maxima(masked):
    best = functools.reduce(jnp.maximum, masked)
    return jnp.max(best.T, axis=0, keepdims=True)


def own_kernel(*refs, rows):
    column, out_ref = refs[:-1], refs[-1]
    out_ref[...] = row_maxima(masked_scores(column[:1], column, rows, True)[0])


def moved_kernel(*refs, rows, turns, lefts):
    column, left, (turn_ref, part_ref) = refs[: -2 - lefts][::-1], refs[-2 - lefts : -2][::-1], refs[-2:]
    masked = masked_scores(left, column, rows, False)
    for t in range(turns):
        turn_ref[t] = row_maxima(masked[t])
    for k in range(len(column)):
        part = functools.reduce(jnp.maximum, [masked[t][k] for t in range(lefts)])
        part_ref[pl.ds(k, 1), :] = jnp.max(part, axis=0, keepdims=True)


def cost(lefts, column):
    cells = column[0].size
    return pl.CostEstimate(
        flops=2 * LANES * lefts * len(column) * cells,
        bytes_accessed=2 * cells * (lefts + len(column)),
        transcendentals=0,
    )


def column_order(count):
    return [0, 2, 1, 3] if count == 4 else list(range(count))


def on_device(embeds, assignment):
    rows = embeds.shape[0]
    columns, lanes = lax.axis_size("dev"), lax.axis_size("sub")
    order = column_order(columns)

    def along_dev(value, step):
        pairs = [(order[i], order[(i + step) % columns]) for i in range(columns)]
        return lax.ppermute(value, "dev", pairs)

    def along_sub(value, flip):
        return lax.ppermute(value, "sub", [(i, i ^ flip) for i in range(lanes)])

    own = pack(embeds, assignment)
    turns = list(range(1, (columns + 1) // 2))
    left = [along_dev(own, step) for step in turns]
    if columns % 2 == 0:
        left.append(along_dev(own, columns // 2))
    column = {0: own}
    for flip in range(2, lanes, 2):
        column[flip] = along_sub(own, flip)
    for flip in range(0, lanes, 2):
        column[flip + 1] = along_sub(column[flip], 1)
    column = [column[k] for k in range(lanes)]

    turn_best, part = pl.pallas_call(
        functools.partial(moved_kernel, rows=rows, turns=len(turns), lefts=len(left)),
        out_shape=[
            jax.ShapeDtypeStruct((len(turns), 1, rows), jnp.float32),
            jax.ShapeDtypeStruct((lanes, rows), jnp.float32),
        ],
        cost_estimate=cost(len(left), column),
        compiler_params=pltpu.CompilerParams(vmem_limit_bytes=VMEM_BYTES),
    )(*column[::-1], *left[::-1])
    own_best = pl.pallas_call(
        functools.partial(own_kernel, rows=rows),
        out_shape=jax.ShapeDtypeStruct((1, rows), jnp.float32),
        cost_estimate=cost(1, column),
        compiler_params=pltpu.CompilerParams(vmem_limit_bytes=VMEM_BYTES),
    )(*column)

    best = [own_best] + [along_dev(turn_best[t], -step) for t, step in enumerate(turns)]
    pair = part[:2]
    for flip in range(2, lanes, 2):
        pair = jnp.maximum(pair, along_sub(part[flip : flip + 2], flip))
    best.append(pair[:1])
    best.append(along_sub(pair[1:], 1))
    return functools.reduce(jnp.maximum, best).reshape(rows)


def solution(mesh):
    placed = (P(("groups", "dev", "sub"), None), P(("groups", "dev", "sub")))
    return jax.shard_map(
        on_device,
        mesh=mesh,
        in_specs=placed,
        out_specs=P(("groups", "dev", "sub")),
        check_vma=False,
    )
```

time: 35 us -> 26.8 us (0.77)
  waiting for transfers between devices: 19.2 us -> 12.8 us
  starting transfers between devices: 11.7 us -> 10.1 us
    ppermute x3, waiting for transfers between devices: 14.1 us -> 10 us  [along_dev(): return lax.ppermute(value, 'dev', pairs)]
    ppermute x5, waiting for transfers between devices: 5.16 us -> 2.83 us  [along_sub(): return lax.ppermute(value, 'sub', [(i, i ^ flip) for i in range(lanes)])]
    ppermute x5, starting transfers between devices: 4.62 us -> 3.55 us  [along_sub(): return lax.ppermute(value, 'sub', [(i, i ^ flip) for i in range(lanes)])]
    ppermute x3, starting transfers between devices: 7.12 us -> 6.6 us  [along_dev(): return lax.ppermute(value, 'dev', pairs)]
  transfers between devices with their start and end apart: 8 -> 8, of which waited for: 4 -> 5; matrix products, arithmetic and copies ran while one was open for 0% -> 0% of each run, Pallas kernels for 3% -> 2%
where the time goes in v2:
time: 26.8 us; the launch traced here: 26.6 us
  waiting for transfers between devices  12.8 us (48%)
  starting transfers between devices  10.1 us (38%)
  local copies, waits for them, and re-layouts  1.7 us (6%)
  Pallas kernels  1.39 us (5%)
  other arithmetic  0.52 us (2%)
    ppermute x3, waiting for transfers between devices, along_dev(): return lax.ppermute(value, 'dev', pairs)  10 us
    ppermute x3, starting transfers between devices, along_dev(): return lax.ppermute(value, 'dev', pairs)  6.6 us
    ppermute x5, starting transfers between devices, along_sub(): return lax.ppermute(value, 'sub', [(i, i ^ flip) for i in range(lanes)])  3.55 us
    ppermute x5, waiting for transfers between devices, along_sub(): return lax.ppermute(value, 'sub', [(i, i ^ flip) for i in range(lanes)])  2.83 us
    unnamed x4, local copies, waits for them, and re-layouts  1.69 us
    pallas_call x1, Pallas kernels, on_device(): pl.pallas_call(functools.partial(moved_kernel, rows=rows, turns=len(turns...  0.75 us
  transfers between devices with their start and end apart: 8, of which 5 were waited for; matrix products, arithmetic and copies ran while one was open for 0% of the time, Pallas kernels for 2%

profile of v2, /device:TPU:0, one launch (start us, length us, event | category | flops | bytes accessed | tf_op | source)
XLA Modules:
  0.0 26.6 jit_solution(2275102151136303750)
XLA Ops:
  0.0 0.0 copy-start
  0.0 1.0 %copy-done = f32[128,1024]{1,0:T(8,128)S(1)} copy-done((f32[128,1024]{1,0:T(8,128)S(1)}, f32[128,1024]{1,0:T(8,128)}, u32[]{:S(2)}) %copy-start) | copy-done | bytes 524312
  1.0 0.1 shard_map.28.packed_ref
  1.2 0.0 copy-start.1
  1.2 0.6 %copy-done.1 = s32[128]{0:T(128)S(1)} copy-done((s32[128]{0:T(128)S(1)}, s32[128]{0:T(128)}, u32[]{:S(2)}) %copy-start.1) | copy-done | bytes 536
  1.8 2.9 %collective-permute-start.1 = (bf16[1040,128]{1,0:T(8,128)(2,1)S(1)}, bf16[1040,128]{1,0:T(8,128)(2,1)S(1)}, u32[]{:S(2)}, u32[]{:S(2)}) collective-permute-start(bf16[1040,128]{1,0:T(8,128)(2,1)S(1)} %shard_map.29.refs_0_.refs_3_), channel_id=1, source_target_pairs={{0,2},{1,3},{2,0},{3,1},{4,6},{5,7},{6,4},{7,5},{8,10},{9,11},{10,... | collective-permute-start | bytes 798728 | tf_op jit(solution)/shard_map/ppermute | solution.py:125
  4.8 2.6 %collective-permute-start.4 = (bf16[1040,128]{1,0:T(8,128)(2,1)S(1)}, bf16[1040,128]{1,0:T(8,128)(2,1)S(1)}, u32[]{:S(2)}, u32[]{:S(2)}) collective-permute-start(bf16[1040,128]{1,0:T(8,128)(2,1)S(1)} %shard_map.29.refs_0_.refs_3_), channel_id=1, source_target_pairs={{0,8},{8,4},{4,12},{12,0},{1,9},{9,5},{5,13},{13,1},{2,10},{10,6},... | collective-permute-start | bytes 798728 | tf_op jit(solution)/shard_map/ppermute | solution.py:122
  7.4 1.6 %collective-permute-start.3 = (bf16[1040,128]{1,0:T(8,128)(2,1)S(1)}, bf16[1040,128]{1,0:T(8,128)(2,1)S(1)}, u32[]{:S(2)}, u32[]{:S(2)}) collective-permute-start(bf16[1040,128]{1,0:T(8,128)(2,1)S(1)} %shard_map.29.refs_0_.refs_3_), channel_id=1, source_target_pairs={{0,4},{8,12},{4,0},{12,8},{1,5},{9,13},{5,1},{13,9},{2,6},{10,14},... | collective-permute-start | bytes 798728 | tf_op jit(solution)/shard_map/ppermute | solution.py:122
  8.9 0.0 collective-permute-start
  8.9 2.2 %collective-permute-done.1.refs_2_.refs_1_ = bf16[1040,128]{1,0:T(8,128)(2,1)S(1)} collective-permute-done((bf16[1040,128]{1,0:T(8,128)(2,1)S(1)}, bf16[1040,128]{1,0:T(8,128)(2,1)S(1)}, u32[]{:S(2)}, u32[]{:S(2)}) %collective-permute-start.1) | collective-permute-done | bytes 266272 | tf_op jit(solution)/shard_map/ppermute | solution.py:125
  11.2 0.0 collective-permute-start.2
  11.2 4.8 %collective-permute-done.4.refs_5_ = bf16[1040,128]{1,0:T(8,128)(2,1)S(1)} collective-permute-done((bf16[1040,128]{1,0:T(8,128)(2,1)S(1)}, bf16[1040,128]{1,0:T(8,128)(2,1)S(1)}, u32[]{:S(2)}, u32[]{:S(2)}) %collective-permute-start.4) | collective-permute-done | bytes 266272 | tf_op jit(solution)/shard_map/ppermute | solution.py:122
  15.9 4.4 %collective-permute-done.3.refs_4_ = bf16[1040,128]{1,0:T(8,128)(2,1)S(1)} collective-permute-done((bf16[1040,128]{1,0:T(8,128)(2,1)S(1)}, bf16[1040,128]{1,0:T(8,128)(2,1)S(1)}, u32[]{:S(2)}, u32[]{:S(2)}) %collective-permute-start.3) | collective-permute-done | bytes 266272 | tf_op jit(solution)/shard_map/ppermute | solution.py:122
  20.3 0.0 collective-permute-done.refs_1_.refs_2_
  20.3 0.0 collective-permute-done.2.refs_3_.refs_0_
  20.3 0.8 %shard_map.31 = (f32[1,1,128]{2,1,0:T(1,128)S(1)}, f32[4,128]{1,0:T(4,128)S(1)}) custom-call(bf16[1040,128]{1,0:T(8,128)(2,1)S(1)} %collective-permute-done.2.refs_3_.refs_0_, bf16[1040,128]{1,0:T(8,128)(2,1)S(1)} %collective-permute-done.1.refs_2_.refs_1_, bf16[1040,128]{1,0:T(8,128)(2,1)S(1)} %collective-permute-done.refs_1_.refs_2_, ...), custom_call_target="tpu_custom_call" | custom-call | flops 272629760 | bytes 1597440 | tf_op jit(solution)/shard_map/pallas_call | solution.py:139
  21.1 0.6 %collective-permute-start.6 = (f32[2,128]{1,0:T(2,128)S(1)}, f32[2,128]{1,0:T(2,128)S(1)}, u32[]{:S(2)}, u32[]{:S(2)}) collective-permute-start(f32[2,128]{1,0:T(2,128)S(1)} %slice.13), channel_id=1, source_target_pairs={{0,2},{1,3},{2,0},{3,1},{4,6},{5,7},{6,4},{7,5},{8,10},{9,11},{10,... | collective-permute-start | bytes 3080 | tf_op jit(solution)/shard_map/ppermute | solution.py:125
  21.7 2.4 %collective-permute-start.5 = (f32[1,128]{1,0:T(1,128)S(1)}, f32[1,128]{1,0:T(1,128)S(1)}, u32[]{:S(2)}, u32[]{:S(2)}) collective-permute-start(f32[1,128]{1,0:T(1,128)S(1)} %bitcast.5), channel_id=1, source_target_pairs={{0,12},{8,0},{4,8},{12,4},{1,13},{9,1},{5,9},{13,5},{2,14},{10,2},... | collective-permute-start | bytes 1544 | tf_op jit(solution)/shard_map/ppermute | solution.py:122
  24.1 0.6 %collective-permute-done.6 = f32[2,128]{1,0:T(2,128)S(1)} collective-permute-done((f32[2,128]{1,0:T(2,128)S(1)}, f32[2,128]{1,0:T(2,128)S(1)}, u32[]{:S(2)}, u32[]{:S(2)}) %collective-permute-start.6) | collective-permute-done | bytes 1056 | tf_op jit(solution)/shard_map/ppermute | solution.py:125
  24.7 0.0 collective-permute-start.7
  24.7 0.5 %shard_map.30 = f32[1,128]{1,0:T(1,128)S(1)} custom-call(bf16[1040,128]{1,0:T(8,128)(2,1)S(1)} %shard_map.29.refs_0_.refs_3_, bf16[1040,128]{1,0:T(8,128)(2,1)S(1)} %collective-permute-done.refs_1_.refs_2_, bf16[1040,128]{1,0:T(8,128)(2,1)S(1)} %collective-permute-done.1.refs_2_.refs_1_, bf16[1040,128]{1,0:T(8,128)(2,1)S(1)} %collective-permute-done.2.refs_3_.refs_0_), custom_call_target="tpu_custom_call" | custom-call | flops 136314880 | bytes 1331200 | tf_op jit(solution)/shard_map/pallas_call | solution.py:148
  25.2 0.9 %collective-permute-done.5 = f32[1,128]{1,0:T(1,128)S(1)} collective-permute-done((f32[1,128]{1,0:T(1,128)S(1)}, f32[1,128]{1,0:T(1,128)S(1)}, u32[]{:S(2)}, u32[]{:S(2)}) %collective-permute-start.5) | collective-permute-done | bytes 544 | tf_op jit(solution)/shard_map/ppermute | solution.py:122
  26.1 0.0 collective-permute-done.7
  26.1 0.5 %maximum_bitcast_fusion = f32[128]{0:T(128)} fusion(f32[1,128]{1,0:T(1,128)S(1)} %collective-permute-done.7, f32[2,128]{1,0:T(2,128)S(1)} %slice_maximum_fusion, f32[1,128]{1,0:T(1,128)S(1)} %shard_map.30, f32[1,128]{1,0:T(1,128)S(1)} %collective-permute-done.5), kind=kLoop, calls=%fused_computation.1 | loop fusion | flops 384 | bytes 2560 | tf_op jit(solution)/shard_map/reshape | solution.py:161
  (4 shorter events, 0.0 us)
Async XLA Ops:
  0.0 1.0 %copy-start = (f32[128,1024]{1,0:T(8,128)S(1)}, f32[128,1024]{1,0:T(8,128)}, u32[]{:S(2)}) copy-start(f32[128,1024]{1,0:T(8,128)} %embeds_ref.1) | copy-start | bytes 1572868
  1.2 0.7 %copy-start.1 = (s32[128]{0:T(128)S(1)}, s32[128]{0:T(128)}, u32[]{:S(2)}) copy-start(s32[128]{0:T(128)} %param.3) | copy-start | bytes 1540
  1.8 9.3 %collective-permute-start.1 = (bf16[1040,128]{1,0:T(8,128)(2,1)S(1)}, bf16[1040,128]{1,0:T(8,128)(2,1)S(1)}, u32[]{:S(2)}, u32[]{:S(2)}) collective-permute-start(bf16[1040,128]{1,0:T(8,128)(2,1)S(1)} %shard_map.29.refs_0_.refs_3_), channel_id=1, source_target_pairs={{0,2},{1,3},{2,0},{3,1},{4,6},{5,7},{6,4},{7,5},{8,10},{9,11},{10,... | collective-permute-start | bytes 798728 | tf_op jit(solution)/shard_map/ppermute | solution.py:125
  4.8 11.2 %collective-permute-start.4 = (bf16[1040,128]{1,0:T(8,128)(2,1)S(1)}, bf16[1040,128]{1,0:T(8,128)(2,1)S(1)}, u32[]{:S(2)}, u32[]{:S(2)}) collective-permute-start(bf16[1040,128]{1,0:T(8,128)(2,1)S(1)} %shard_map.29.refs_0_.refs_3_), channel_id=1, source_target_pairs={{0,8},{8,4},{4,12},{12,0},{1,9},{9,5},{5,13},{13,1},{2,10},{10,6},... | collective-permute-start | bytes 798728 | tf_op jit(solution)/shard_map/ppermute | solution.py:122
  7.4 12.9 %collective-permute-start.3 = (bf16[1040,128]{1,0:T(8,128)(2,1)S(1)}, bf16[1040,128]{1,0:T(8,128)(2,1)S(1)}, u32[]{:S(2)}, u32[]{:S(2)}) collective-permute-start(bf16[1040,128]{1,0:T(8,128)(2,1)S(1)} %shard_map.29.refs_0_.refs_3_), channel_id=1, source_target_pairs={{0,4},{8,12},{4,0},{12,8},{1,5},{9,13},{5,1},{13,9},{2,6},{10,14},... | collective-permute-start | bytes 798728 | tf_op jit(solution)/shard_map/ppermute | solution.py:122
  8.9 11.4 %collective-permute-start = (bf16[1040,128]{1,0:T(8,128)(2,1)S(1)}, bf16[1040,128]{1,0:T(8,128)(2,1)S(1)}, u32[]{:S(2)}, u32[]{:S(2)}) collective-permute-start(bf16[1040,128]{1,0:T(8,128)(2,1)S(1)} %shard_map.29.refs_0_.refs_3_), channel_id=1, source_target_pairs={{0,1},{1,0},{2,3},{3,2},{4,5},{5,4},{6,7},{7,6},{8,9},{9,8},{10,11... | collective-permute-start | bytes 798728 | tf_op jit(solution)/shard_map/ppermute | solution.py:125
  11.2 9.1 %collective-permute-start.2 = (bf16[1040,128]{1,0:T(8,128)(2,1)S(1)}, bf16[1040,128]{1,0:T(8,128)(2,1)S(1)}, u32[]{:S(2)}, u32[]{:S(2)}) collective-permute-start(bf16[1040,128]{1,0:T(8,128)(2,1)S(1)} %collective-permute-done.1.refs_2_.refs_1_), channel_id=1, source_target_pairs={{0,1},{1,0},{2,3},{3,2},{4,5},{5,4},{6,7},{7,6},{8,9},{9,8},{10,11... | collective-permute-start | bytes 798728 | tf_op jit(solution)/shard_map/ppermute | solution.py:125
  21.1 3.6 %collective-permute-start.6 = (f32[2,128]{1,0:T(2,128)S(1)}, f32[2,128]{1,0:T(2,128)S(1)}, u32[]{:S(2)}, u32[]{:S(2)}) collective-permute-start(f32[2,128]{1,0:T(2,128)S(1)} %slice.13), channel_id=1, source_target_pairs={{0,2},{1,3},{2,0},{3,1},{4,6},{5,7},{6,4},{7,5},{8,10},{9,11},{10,... | collective-permute-start | bytes 3080 | tf_op jit(solution)/shard_map/ppermute | solution.py:125
  21.7 4.4 %collective-permute-start.5 = (f32[1,128]{1,0:T(1,128)S(1)}, f32[1,128]{1,0:T(1,128)S(1)}, u32[]{:S(2)}, u32[]{:S(2)}) collective-permute-start(f32[1,128]{1,0:T(1,128)S(1)} %bitcast.5), channel_id=1, source_target_pairs={{0,12},{8,0},{4,8},{12,4},{1,13},{9,1},{5,9},{13,5},{2,14},{10,2},... | collective-permute-start | bytes 1544 | tf_op jit(solution)/shard_map/ppermute | solution.py:122
  24.7 1.4 %collective-permute-start.7 = (f32[1,128]{1,0:T(1,128)S(1)}, f32[1,128]{1,0:T(1,128)S(1)}, u32[]{:S(2)}, u32[]{:S(2)}) collective-permute-start(f32[1,128]{1,0:T(1,128)S(1)} %slice.15), channel_id=1, source_target_pairs={{0,1},{1,0},{2,3},{3,2},{4,5},{5,4},{6,7},{7,6},{8,9},{9,8},{10,11... | collective-permute-start | bytes 1544 | tf_op jit(solution)/shard_map/ppermute | solution.py:125

commit v3 on v2

--- a/solution.py
+++ b/solution.py
@@ -10,40 +10,59 @@
 LANES = 128
 ID_ROWS = 16
 LOWEST = -1.0
+CHUNKS = 1
 VMEM_BYTES = 16 * 1024 * 1024
 
 
-def pack_kernel(embeds_ref, out_ref):
+def pack_kernel(embeds_hbm, ids_hbm, out_ref, embeds_ref, ids_ref, embeds_sems, ids_sem):
     rows, width = embeds_ref.shape
-    embeds = embeds_ref[...]
-    squares = jnp.sum(embeds * embeds, axis=1, keepdims=True)
-    unit = (embeds * lax.rsqrt(squares + 1e-06)).astype(jnp.bfloat16)
-    for block in range(width // LANES):
-        out_ref[pl.ds(block * rows, rows), :] = unit[:, block * LANES : (block + 1) * LANES]
-
-
-def label_kernel(packed_ref, ids_ref, out_ref):
-    del packed_ref
-    start = out_ref.shape[0] - ID_ROWS
-    ids = jnp.broadcast_to(ids_ref[...].astype(jnp.float32), (ID_ROWS, ids_ref.shape[1]))
-    out_ref[pl.ds(start, ID_ROWS), :] = ids.astype(jnp.bfloat16)
+    some = rows // CHUNKS
+    copies = [
+        pltpu.make_async_copy(
+            embeds_hbm.at[pl.ds(c * some, some), :],
+            embeds_ref.at[pl.ds(c * some, some), :],
+            embeds_sems.at[c],
+        )
+        for c in range(CHUNKS)
+    ]
+    copy_ids = pltpu.make_async_copy(ids_hbm, ids_ref, ids_sem)
+    copy_ids.start()
+    for copy in copies:
+        copy.start()
+    copy_ids.wait()
+    ids = ids_ref[...].astype(jnp.float32)
+    out_ref[pl.ds(width // LANES * rows, ID_ROWS), :] = jnp.broadcast_to(
+        ids, (ID_ROWS, rows)
+    ).astype(jnp.bfloat16)
+    for c, copy in enumerate(copies):
+        copy.wait()
+        embeds = embeds_ref[pl.ds(c * some, some), :]
+        squares = jnp.sum(embeds * embeds, axis=1, keepdims=True)
+        unit = (embeds * lax.rsqrt(squares + 1e-06)).astype(jnp.bfloat16)
+        for block in range(width // LANES):
+            out_ref[pl.ds(block * rows + c * some, some), :] = unit[
+                :, block * LANES : (block + 1) * LANES
+            ]
 
 
 def pack(embeds, ids):
     rows, width = embeds.shape
-    cells = width // LANES * rows
-    shape = jax.ShapeDtypeStruct((cells + ID_ROWS, LANES), jnp.bfloat16)
-    packed = pl.pallas_call(
+    operands = [
+        pltpu.with_memory_space_constraint(value, pltpu.HBM)
+        for value in (embeds, ids.reshape(1, rows))
+    ]
+    return pl.pallas_call(
         pack_kernel,
-        out_shape=shape,
+        out_shape=jax.ShapeDtypeStruct((width // LANES * rows + ID_ROWS, LANES), jnp.bfloat16),
+        in_specs=[pl.BlockSpec(memory_space=pltpu.HBM)] * 2,
+        scratch_shapes=[
+            pltpu.VMEM((rows, width), jnp.float32),
+            pltpu.VMEM((1, rows), jnp.int32),
+            pltpu.SemaphoreType.DMA((CHUNKS,)),
+            pltpu.SemaphoreType.DMA,
+        ],
         compiler_params=pltpu.CompilerParams(vmem_limit_bytes=VMEM_BYTES),
-    )(embeds)
-    return pl.pallas_call(
-        label_kernel,
-        out_shape=shape,
-        input_output_aliases={0: 0},
-        compiler_params=pltpu.CompilerParams(vmem_limit_bytes=VMEM_BYTES),
-    )(packed, ids.reshape(1, rows))
+    )(*operands)
 
 
 def load_rows(ref, rows):
@@ -84,18 +103,20 @@
     return jnp.max(best.T, axis=0, keepdims=True)
 
 
-def own_kernel(*refs, rows):
-    column, out_ref = refs[:-1], refs[-1]
-    out_ref[...] = row_maxima(masked_scores(column[:1], column, rows, True)[0])
+def own_kernel(*refs, rows, place):
+    column = [refs[i] for i in place["column"]]
+    refs[-1][...] = row_maxima(masked_scores(column[:1], column, rows, True)[0])
 
 
-def moved_kernel(*refs, rows, turns, lefts):
-    column, left, (turn_ref, part_ref) = refs[: -2 - lefts][::-1], refs[-2 - lefts : -2][::-1], refs[-2:]
+def moved_kernel(*refs, rows, place):
+    left = [refs[i] for i in place["left"]]
+    column = [refs[i] for i in place["column"]]
+    turn_ref, part_ref = refs[-2:]
     masked = masked_scores(left, column, rows, False)
-    for t in range(turns):
+    for t in range(turn_ref.shape[0]):
         turn_ref[t] = row_maxima(masked[t])
     for k in range(len(column)):
-        part = functools.reduce(jnp.maximum, [masked[t][k] for t in range(lefts)])
+        part = functools.reduce(jnp.maximum, [masked[t][k] for t in range(len(left))])
         part_ref[pl.ds(k, 1), :] = jnp.max(part, axis=0, keepdims=True)
 
 
@@ -129,28 +150,33 @@
     left = [along_dev(own, step) for step in turns]
     if columns % 2 == 0:
         left.append(along_dev(own, columns // 2))
-    column = {0: own}
-    for flip in range(2, lanes, 2):
-        column[flip] = along_sub(own, flip)
-    for flip in range(0, lanes, 2):
-        column[flip + 1] = along_sub(column[flip], 1)
-    column = [column[k] for k in range(lanes)]
+    column = [own] + [along_sub(own, flip) for flip in range(1, lanes)]
 
+    named = [(("left", t), value) for t, value in enumerate(left)]
+    named += [(("column", k), value) for k, value in enumerate(column)]
+    first = [('left', 0), ('column', 2), ('left', 1), ('column', 3), ('column', 1)]
+    named.sort(key=lambda item: -first.index(item[0]) if item[0] in first else 1)
+    blocks = [value for _, value in named]
+    names = [name for name, _ in named]
+    place = {
+        "left": [names.index(("left", t)) for t in range(len(left))],
+        "column": [names.index(("column", k)) for k in range(lanes)],
+    }
     turn_best, part = pl.pallas_call(
-        functools.partial(moved_kernel, rows=rows, turns=len(turns), lefts=len(left)),
+        functools.partial(moved_kernel, rows=rows, place=place),
         out_shape=[
             jax.ShapeDtypeStruct((len(turns), 1, rows), jnp.float32),
             jax.ShapeDtypeStruct((lanes, rows), jnp.float32),
         ],
         cost_estimate=cost(len(left), column),
         compiler_params=pltpu.CompilerParams(vmem_limit_bytes=VMEM_BYTES),
-    )(*column[::-1], *left[::-1])
+    )(*blocks)
     own_best = pl.pallas_call(
-        functools.partial(own_kernel, rows=rows),
+        functools.partial(own_kernel, rows=rows, place=place),
         out_shape=jax.ShapeDtypeStruct((1, rows), jnp.float32),
         cost_estimate=cost(1, column),
         compiler_params=pltpu.CompilerParams(vmem_limit_bytes=VMEM_BYTES),
-    )(*column)
+    )(*blocks)
 
     best = [own_best] + [along_dev(turn_best[t], -step) for t, step in enumerate(turns)]
     pair = part[:2]

time: 26.8 us -> 25.9 us (0.966)
  waiting for transfers between devices: 12.8 us -> 10.9 us
  starting transfers between devices: 10.1 us -> 11.9 us
  local copies, waits for them, and re-layouts: 1.7 us -> 0.01 us
  Pallas kernels: 1.39 us -> 2.46 us
    ppermute x5, waiting for transfers between devices: 2.83 us -> 1 us  [along_sub(): return lax.ppermute(value, 'sub', [(i, i ^ flip) for i in range(lanes)])]
    unnamed x4 -> x0, local copies, waits for them, and re-layouts: 1.69 us -> none
    ppermute x3, starting transfers between devices: 6.6 us -> 8.11 us  [along_dev(): return lax.ppermute(value, 'dev', pairs)]
    pallas_call x4 -> x3, Pallas kernels: 1.39 us -> 2.46 us  [the longest x1 1.2 us: pack(): pl.pallas_call(pack_kernel, out_shape=jax.ShapeDtypeStruct((width // LANE...]
  transfers between devices with their start and end apart: 8 -> 8, of which waited for: 5 -> 4; matrix products, arithmetic and copies ran while one was open for 0% -> 0% of each run, Pallas kernels for 2% -> 2%
where the time goes in v3:
time: 25.9 us; the launch traced here: 25.8 us
  starting transfers between devices  11.9 us (46%)
  waiting for transfers between devices  10.9 us (42%)
  Pallas kernels  2.46 us (9%)
  other arithmetic  0.52 us (2%)
    ppermute x3, waiting for transfers between devices, along_dev(): return lax.ppermute(value, 'dev', pairs)  9.89 us
    ppermute x3, starting transfers between devices, along_dev(): return lax.ppermute(value, 'dev', pairs)  8.11 us
    ppermute x5, starting transfers between devices, along_sub(): return lax.ppermute(value, 'sub', [(i, i ^ flip) for i in range(lanes)])  3.77 us
    pallas_call x1, Pallas kernels, pack(): pl.pallas_call(pack_kernel, out_shape=jax.ShapeDtypeStruct((width // LANE...  1.2 us
    ppermute x5, waiting for transfers between devices, along_sub(): return lax.ppermute(value, 'sub', [(i, i ^ flip) for i in range(lanes)])  1 us
    pallas_call x1, Pallas kernels, on_device(): pl.pallas_call(functools.partial(moved_kernel, rows=rows, place=place), o...  0.76 us
  transfers between devices with their start and end apart: 8, of which 4 were waited for; matrix products, arithmetic and copies ran while one was open for 0% of the time, Pallas kernels for 2%

profile of v3, /device:TPU:0, one launch (start us, length us, event | category | flops | bytes accessed | tf_op | source)
XLA Modules:
  0.0 25.8 jit_solution(3426447628847823370)
XLA Ops:
  0.0 1.2 %shard_map.28.refs_5_ = bf16[1040,128]{1,0:T(8,128)(2,1)S(1)} custom-call(f32[128,1024]{1,0:T(8,128)} %embeds_hbm.1, s32[1,128]{1,0:T(1,128)} %bitcast.5), custom_call_target="tpu_custom_call" | custom-call | tf_op jit(solution)/shard_map/pallas_call | solution.py:54
  1.2 4.1 %collective-permute-start.4 = (bf16[1040,128]{1,0:T(8,128)(2,1)S(1)}, bf16[1040,128]{1,0:T(8,128)(2,1)S(1)}, u32[]{:S(2)}, u32[]{:S(2)}) collective-permute-start(bf16[1040,128]{1,0:T(8,128)(2,1)S(1)} %shard_map.28.refs_5_), channel_id=1, source_target_pairs={{0,8},{8,4},{4,12},{12,0},{1,9},{9,5},{5,13},{13,1},{2,10},{10,6},... | collective-permute-start | bytes 798728 | tf_op jit(solution)/shard_map/ppermute | solution.py:143
  5.3 1.5 %collective-permute-start.3 = (bf16[1040,128]{1,0:T(8,128)(2,1)S(1)}, bf16[1040,128]{1,0:T(8,128)(2,1)S(1)}, u32[]{:S(2)}, u32[]{:S(2)}) collective-permute-start(bf16[1040,128]{1,0:T(8,128)(2,1)S(1)} %shard_map.28.refs_5_), channel_id=1, source_target_pairs={{0,2},{1,3},{2,0},{3,1},{4,6},{5,7},{6,4},{7,5},{8,10},{9,11},{10,... | collective-permute-start | bytes 798728 | tf_op jit(solution)/shard_map/ppermute | solution.py:146
  6.8 1.6 %collective-permute-start.2 = (bf16[1040,128]{1,0:T(8,128)(2,1)S(1)}, bf16[1040,128]{1,0:T(8,128)(2,1)S(1)}, u32[]{:S(2)}, u32[]{:S(2)}) collective-permute-start(bf16[1040,128]{1,0:T(8,128)(2,1)S(1)} %shard_map.28.refs_5_), channel_id=1, source_target_pairs={{0,4},{8,12},{4,0},{12,8},{1,5},{9,13},{5,1},{13,9},{2,6},{10,14},... | collective-permute-start | bytes 798728 | tf_op jit(solution)/shard_map/ppermute | solution.py:143
  8.4 0.0 collective-permute-start.1
  8.4 0.6 %collective-permute-start = (bf16[1040,128]{1,0:T(8,128)(2,1)S(1)}, bf16[1040,128]{1,0:T(8,128)(2,1)S(1)}, u32[]{:S(2)}, u32[]{:S(2)}) collective-permute-start(bf16[1040,128]{1,0:T(8,128)(2,1)S(1)} %shard_map.28.refs_5_), channel_id=1, source_target_pairs={{0,1},{1,0},{2,3},{3,2},{4,5},{5,4},{6,7},{7,6},{8,9},{9,8},{10,11... | collective-permute-start | bytes 798728 | tf_op jit(solution)/shard_map/ppermute | solution.py:146
  9.0 4.6 %collective-permute-done.4.refs_4_ = bf16[1040,128]{1,0:T(8,128)(2,1)S(1)} collective-permute-done((bf16[1040,128]{1,0:T(8,128)(2,1)S(1)}, bf16[1040,128]{1,0:T(8,128)(2,1)S(1)}, u32[]{:S(2)}, u32[]{:S(2)}) %collective-permute-start.4) | collective-permute-done | bytes 266272 | tf_op jit(solution)/shard_map/ppermute | solution.py:143
  13.6 1.0 %collective-permute-done.3.refs_3_ = bf16[1040,128]{1,0:T(8,128)(2,1)S(1)} collective-permute-done((bf16[1040,128]{1,0:T(8,128)(2,1)S(1)}, bf16[1040,128]{1,0:T(8,128)(2,1)S(1)}, u32[]{:S(2)}, u32[]{:S(2)}) %collective-permute-start.3) | collective-permute-done | bytes 266272 | tf_op jit(solution)/shard_map/ppermute | solution.py:146
  14.6 3.9 %collective-permute-done.2.refs_2_ = bf16[1040,128]{1,0:T(8,128)(2,1)S(1)} collective-permute-done((bf16[1040,128]{1,0:T(8,128)(2,1)S(1)}, bf16[1040,128]{1,0:T(8,128)(2,1)S(1)}, u32[]{:S(2)}, u32[]{:S(2)}) %collective-permute-start.2) | collective-permute-done | bytes 266272 | tf_op jit(solution)/shard_map/ppermute | solution.py:143
  18.5 0.0 collective-permute-done.1.refs_1_
  18.5 0.0 collective-permute-done.refs_0_
  18.5 0.8 %shard_map.30 = (f32[1,1,128]{2,1,0:T(1,128)S(1)}, f32[4,128]{1,0:T(4,128)S(1)}) custom-call(bf16[1040,128]{1,0:T(8,128)(2,1)S(1)} %collective-permute-done.refs_0_, bf16[1040,128]{1,0:T(8,128)(2,1)S(1)} %collective-permute-done.1.refs_1_, bf16[1040,128]{1,0:T(8,128)(2,1)S(1)} %collective-permute-done.2.refs_2_, ...), custom_call_target="tpu_custom_call" | custom-call | flops 272629760 | bytes 1597440 | tf_op jit(solution)/shard_map/pallas_call | solution.py:165
  19.3 1.6 %collective-permute-start.6 = (f32[2,128]{1,0:T(2,128)S(1)}, f32[2,128]{1,0:T(2,128)S(1)}, u32[]{:S(2)}, u32[]{:S(2)}) collective-permute-start(f32[2,128]{1,0:T(2,128)S(1)} %slice.13), channel_id=1, source_target_pairs={{0,2},{1,3},{2,0},{3,1},{4,6},{5,7},{6,4},{7,5},{8,10},{9,11},{10,... | collective-permute-start | bytes 3080 | tf_op jit(solution)/shard_map/ppermute | solution.py:146
  20.8 2.4 %collective-permute-start.5 = (f32[1,128]{1,0:T(1,128)S(1)}, f32[1,128]{1,0:T(1,128)S(1)}, u32[]{:S(2)}, u32[]{:S(2)}) collective-permute-start(f32[1,128]{1,0:T(1,128)S(1)} %bitcast.4), channel_id=1, source_target_pairs={{0,12},{8,0},{4,8},{12,4},{1,13},{9,1},{5,9},{13,5},{2,14},{10,2},... | collective-permute-start | bytes 1544 | tf_op jit(solution)/shard_map/ppermute | solution.py:143
  23.3 0.0 collective-permute-done.6
  23.3 0.1 collective-permute-start.7
  23.4 0.5 %shard_map.29 = f32[1,128]{1,0:T(1,128)S(1)} custom-call(bf16[1040,128]{1,0:T(8,128)(2,1)S(1)} %collective-permute-done.refs_0_, bf16[1040,128]{1,0:T(8,128)(2,1)S(1)} %collective-permute-done.1.refs_1_, bf16[1040,128]{1,0:T(8,128)(2,1)S(1)} %collective-permute-done.2.refs_2_, bf16[1040,128]{1,0:T(8,128)(2,1)S(1)} %collective-permute-done.3.refs_3_, ...), custom_call_target="tpu_custom_call" | custom-call | flops 136314880 | bytes 1331200 | tf_op jit(solution)/shard_map/pallas_call | solution.py:174
  23.9 1.4 %collective-permute-done.5 = f32[1,128]{1,0:T(1,128)S(1)} collective-permute-done((f32[1,128]{1,0:T(1,128)S(1)}, f32[1,128]{1,0:T(1,128)S(1)}, u32[]{:S(2)}, u32[]{:S(2)}) %collective-permute-start.5) | collective-permute-done | bytes 544 | tf_op jit(solution)/shard_map/ppermute | solution.py:143
  25.3 0.0 collective-permute-done.7
  25.3 0.5 %maximum_bitcast_fusion = f32[128]{0:T(128)} fusion(f32[1,128]{1,0:T(1,128)S(1)} %collective-permute-done.7, f32[2,128]{1,0:T(2,128)S(1)} %slice_maximum_fusion, f32[1,128]{1,0:T(1,128)S(1)} %shard_map.29, f32[1,128]{1,0:T(1,128)S(1)} %collective-permute-done.5), kind=kLoop, calls=%fused_computation.1 | loop fusion | flops 384 | bytes 2560 | tf_op jit(solution)/shard_map/reshape | solution.py:187
  (3 shorter events, 0.0 us)
Async XLA Ops:
  1.2 12.4 %collective-permute-start.4 = (bf16[1040,128]{1,0:T(8,128)(2,1)S(1)}, bf16[1040,128]{1,0:T(8,128)(2,1)S(1)}, u32[]{:S(2)}, u32[]{:S(2)}) collective-permute-start(bf16[1040,128]{1,0:T(8,128)(2,1)S(1)} %shard_map.28.refs_5_), channel_id=1, source_target_pairs={{0,8},{8,4},{4,12},{12,0},{1,9},{9,5},{5,13},{13,1},{2,10},{10,6},... | collective-permute-start | bytes 798728 | tf_op jit(solution)/shard_map/ppermute | solution.py:143
  5.3 9.3 %collective-permute-start.3 = (bf16[1040,128]{1,0:T(8,128)(2,1)S(1)}, bf16[1040,128]{1,0:T(8,128)(2,1)S(1)}, u32[]{:S(2)}, u32[]{:S(2)}) collective-permute-start(bf16[1040,128]{1,0:T(8,128)(2,1)S(1)} %shard_map.28.refs_5_), channel_id=1, source_target_pairs={{0,2},{1,3},{2,0},{3,1},{4,6},{5,7},{6,4},{7,5},{8,10},{9,11},{10,... | collective-permute-start | bytes 798728 | tf_op jit(solution)/shard_map/ppermute | solution.py:146
  6.8 11.7 %collective-permute-start.2 = (bf16[1040,128]{1,0:T(8,128)(2,1)S(1)}, bf16[1040,128]{1,0:T(8,128)(2,1)S(1)}, u32[]{:S(2)}, u32[]{:S(2)}) collective-permute-start(bf16[1040,128]{1,0:T(8,128)(2,1)S(1)} %shard_map.28.refs_5_), channel_id=1, source_target_pairs={{0,4},{8,12},{4,0},{12,8},{1,5},{9,13},{5,1},{13,9},{2,6},{10,14},... | collective-permute-start | bytes 798728 | tf_op jit(solution)/shard_map/ppermute | solution.py:143
  8.4 10.1 %collective-permute-start.1 = (bf16[1040,128]{1,0:T(8,128)(2,1)S(1)}, bf16[1040,128]{1,0:T(8,128)(2,1)S(1)}, u32[]{:S(2)}, u32[]{:S(2)}) collective-permute-start(bf16[1040,128]{1,0:T(8,128)(2,1)S(1)} %shard_map.28.refs_5_), channel_id=1, source_target_pairs={{0,3},{1,2},{2,1},{3,0},{4,7},{5,6},{6,5},{7,4},{8,11},{9,10},{10,... | collective-permute-start | bytes 798728 | tf_op jit(solution)/shard_map/ppermute | solution.py:146
  8.4 10.1 %collective-permute-start = (bf16[1040,128]{1,0:T(8,128)(2,1)S(1)}, bf16[1040,128]{1,0:T(8,128)(2,1)S(1)}, u32[]{:S(2)}, u32[]{:S(2)}) collective-permute-start(bf16[1040,128]{1,0:T(8,128)(2,1)S(1)} %shard_map.28.refs_5_), channel_id=1, source_target_pairs={{0,1},{1,0},{2,3},{3,2},{4,5},{5,4},{6,7},{7,6},{8,9},{9,8},{10,11... | collective-permute-start | bytes 798728 | tf_op jit(solution)/shard_map/ppermute | solution.py:146
  19.3 4.0 %collective-permute-start.6 = (f32[2,128]{1,0:T(2,128)S(1)}, f32[2,128]{1,0:T(2,128)S(1)}, u32[]{:S(2)}, u32[]{:S(2)}) collective-permute-start(f32[2,128]{1,0:T(2,128)S(1)} %slice.13), channel_id=1, source_target_pairs={{0,2},{1,3},{2,0},{3,1},{4,6},{5,7},{6,4},{7,5},{8,10},{9,11},{10,... | collective-permute-start | bytes 3080 | tf_op jit(solution)/shard_map/ppermute | solution.py:146
  20.8 4.4 %collective-permute-start.5 = (f32[1,128]{1,0:T(1,128)S(1)}, f32[1,128]{1,0:T(1,128)S(1)}, u32[]{:S(2)}, u32[]{:S(2)}) collective-permute-start(f32[1,128]{1,0:T(1,128)S(1)} %bitcast.4), channel_id=1, source_target_pairs={{0,12},{8,0},{4,8},{12,4},{1,13},{9,1},{5,9},{13,5},{2,14},{10,2},... | collective-permute-start | bytes 1544 | tf_op jit(solution)/shard_map/ppermute | solution.py:143
  23.3 2.0 %collective-permute-start.7 = (f32[1,128]{1,0:T(1,128)S(1)}, f32[1,128]{1,0:T(1,128)S(1)}, u32[]{:S(2)}, u32[]{:S(2)}) collective-permute-start(f32[1,128]{1,0:T(1,128)S(1)} %slice.15), channel_id=1, source_target_pairs={{0,1},{1,0},{2,3},{3,2},{4,5},{5,4},{6,7},{7,6},{8,9},{9,8},{10,11... | collective-permute-start | bytes 1544 | tf_op jit(solution)/shard_map/ppermute | solution.py:146

commit v4 on v3

--- a/solution.py
+++ b/solution.py
@@ -79,22 +79,24 @@
     left = jnp.concatenate([load_rows(ref, rows) for ref in left_refs], axis=0)
     left_ids = [jnp.broadcast_to(load_ids(ref), (rows, rows)).T for ref in left_refs]
     masked = [[] for _ in left_refs]
-    for k, ref in enumerate(column_refs):
+    for start in range(0, len(column_refs), 4):
+        refs = column_refs[start : start + 4]
         scores = lax.dot_general(
             left,
-            load_rows(ref, rows),
+            jnp.concatenate([load_rows(ref, rows) for ref in refs], axis=0),
             (((1,), (1,)), ((), ())),
             preferred_element_type=jnp.float32,
         )
-        ids = load_ids(ref)
-        for t in range(len(left_refs)):
-            same = left_ids[t] == ids
-            if own and k == 0:
-                down = lax.broadcasted_iota(jnp.int32, (rows, rows), 0)
-                across = lax.broadcasted_iota(jnp.int32, (rows, rows), 1)
-                same = same & (down != across)
-            part = scores[t * rows : (t + 1) * rows, :]
-            masked[t].append(jnp.where(same, part, jnp.float32(LOWEST)))
+        for j, ref in enumerate(refs):
+            ids = load_ids(ref)
+            for t in range(len(left_refs)):
+                same = left_ids[t] == ids
+                if own and start + j == 0:
+                    down = lax.broadcasted_iota(jnp.int32, (rows, rows), 0)
+                    across = lax.broadcasted_iota(jnp.int32, (rows, rows), 1)
+                    same = same & (down != across)
+                part = scores[t * rows : (t + 1) * rows, j * rows : (j + 1) * rows]
+                masked[t].append(jnp.where(same, part, jnp.float32(LOWEST)))
     return masked
 
 

time: 25.9 us -> 25.7 us (level)
  no operation moved by 1% of the time
where the time goes in v4:
time: 25.7 us; the launch traced here: 25.6 us
  starting transfers between devices  11.9 us (46%)
  waiting for transfers between devices  10.9 us (42%)
  Pallas kernels  2.26 us (9%)
  other arithmetic  0.52 us (2%)
    ppermute x3, waiting for transfers between devices, along_dev(): return lax.ppermute(value, 'dev', pairs)  9.86 us
    ppermute x3, starting transfers between devices, along_dev(): return lax.ppermute(value, 'dev', pairs)  8.1 us
    ppermute x5, starting transfers between devices, along_sub(): return lax.ppermute(value, 'sub', [(i, i ^ flip) for i in range(lanes)])  3.77 us
    pallas_call x1, Pallas kernels, pack(): pl.pallas_call(pack_kernel, out_shape=jax.ShapeDtypeStruct((width // LANE...  1.2 us
    ppermute x5, waiting for transfers between devices, along_sub(): return lax.ppermute(value, 'sub', [(i, i ^ flip) for i in range(lanes)])  1 us
    pallas_call x1, Pallas kernels, on_device(): pl.pallas_call(functools.partial(own_kernel, rows=rows, place=place), out...  0.54 us
    pallas_call x1, Pallas kernels, on_device(): pl.pallas_call(functools.partial(moved_kernel, rows=rows, place=place), o...  0.52 us
    reshape x1, other arithmetic, on_device(): return functools.reduce(jnp.maximum, best).reshape(rows)  0.52 us
  transfers between devices with their start and end apart: 8, of which 4 were waited for; matrix products, arithmetic and copies ran while one was open for 0% of the time, Pallas kernels for 2%

profile of v4, /device:TPU:0, one launch (start us, length us, event | category | flops | bytes accessed | tf_op | source)
XLA Modules:
  0.0 25.6 jit_solution(13891457270322171321)
XLA Ops:
  0.0 1.2 %shard_map.28.refs_5_ = bf16[1040,128]{1,0:T(8,128)(2,1)S(1)} custom-call(f32[128,1024]{1,0:T(8,128)} %embeds_hbm.1, s32[1,128]{1,0:T(1,128)} %bitcast.5), custom_call_target="tpu_custom_call" | custom-call | tf_op jit(solution)/shard_map/pallas_call | solution.py:54
  1.2 4.1 %collective-permute-start.4 = (bf16[1040,128]{1,0:T(8,128)(2,1)S(1)}, bf16[1040,128]{1,0:T(8,128)(2,1)S(1)}, u32[]{:S(2)}, u32[]{:S(2)}) collective-permute-start(bf16[1040,128]{1,0:T(8,128)(2,1)S(1)} %shard_map.28.refs_5_), channel_id=1, source_target_pairs={{0,8},{8,4},{4,12},{12,0},{1,9},{9,5},{5,13},{13,1},{2,10},{10,6},... | collective-permute-start | bytes 798728 | tf_op jit(solution)/shard_map/ppermute | solution.py:145
  5.3 1.5 %collective-permute-start.3 = (bf16[1040,128]{1,0:T(8,128)(2,1)S(1)}, bf16[1040,128]{1,0:T(8,128)(2,1)S(1)}, u32[]{:S(2)}, u32[]{:S(2)}) collective-permute-start(bf16[1040,128]{1,0:T(8,128)(2,1)S(1)} %shard_map.28.refs_5_), channel_id=1, source_target_pairs={{0,2},{1,3},{2,0},{3,1},{4,6},{5,7},{6,4},{7,5},{8,10},{9,11},{10,... | collective-permute-start | bytes 798728 | tf_op jit(solution)/shard_map/ppermute | solution.py:148
  6.8 1.6 %collective-permute-start.2 = (bf16[1040,128]{1,0:T(8,128)(2,1)S(1)}, bf16[1040,128]{1,0:T(8,128)(2,1)S(1)}, u32[]{:S(2)}, u32[]{:S(2)}) collective-permute-start(bf16[1040,128]{1,0:T(8,128)(2,1)S(1)} %shard_map.28.refs_5_), channel_id=1, source_target_pairs={{0,4},{8,12},{4,0},{12,8},{1,5},{9,13},{5,1},{13,9},{2,6},{10,14},... | collective-permute-start | bytes 798728 | tf_op jit(solution)/shard_map/ppermute | solution.py:145
  8.4 0.0 collective-permute-start.1
  8.4 0.6 %collective-permute-start = (bf16[1040,128]{1,0:T(8,128)(2,1)S(1)}, bf16[1040,128]{1,0:T(8,128)(2,1)S(1)}, u32[]{:S(2)}, u32[]{:S(2)}) collective-permute-start(bf16[1040,128]{1,0:T(8,128)(2,1)S(1)} %shard_map.28.refs_5_), channel_id=1, source_target_pairs={{0,1},{1,0},{2,3},{3,2},{4,5},{5,4},{6,7},{7,6},{8,9},{9,8},{10,11... | collective-permute-start | bytes 798728 | tf_op jit(solution)/shard_map/ppermute | solution.py:148
  9.0 4.6 %collective-permute-done.4.refs_4_ = bf16[1040,128]{1,0:T(8,128)(2,1)S(1)} collective-permute-done((bf16[1040,128]{1,0:T(8,128)(2,1)S(1)}, bf16[1040,128]{1,0:T(8,128)(2,1)S(1)}, u32[]{:S(2)}, u32[]{:S(2)}) %collective-permute-start.4) | collective-permute-done | bytes 266272 | tf_op jit(solution)/shard_map/ppermute | solution.py:145
  13.6 1.0 %collective-permute-done.3.refs_3_ = bf16[1040,128]{1,0:T(8,128)(2,1)S(1)} collective-permute-done((bf16[1040,128]{1,0:T(8,128)(2,1)S(1)}, bf16[1040,128]{1,0:T(8,128)(2,1)S(1)}, u32[]{:S(2)}, u32[]{:S(2)}) %collective-permute-start.3) | collective-permute-done | bytes 266272 | tf_op jit(solution)/shard_map/ppermute | solution.py:148
  14.6 3.9 %collective-permute-done.2.refs_2_ = bf16[1040,128]{1,0:T(8,128)(2,1)S(1)} collective-permute-done((bf16[1040,128]{1,0:T(8,128)(2,1)S(1)}, bf16[1040,128]{1,0:T(8,128)(2,1)S(1)}, u32[]{:S(2)}, u32[]{:S(2)}) %collective-permute-start.2) | collective-permute-done | bytes 266272 | tf_op jit(solution)/shard_map/ppermute | solution.py:145
  18.5 0.0 collective-permute-done.1.refs_1_
  18.5 0.0 collective-permute-done.refs_0_
  18.5 0.5 %shard_map.30 = (f32[1,1,128]{2,1,0:T(1,128)S(1)}, f32[4,128]{1,0:T(4,128)S(1)}) custom-call(bf16[1040,128]{1,0:T(8,128)(2,1)S(1)} %collective-permute-done.refs_0_, bf16[1040,128]{1,0:T(8,128)(2,1)S(1)} %collective-permute-done.1.refs_1_, bf16[1040,128]{1,0:T(8,128)(2,1)S(1)} %collective-permute-done.2.refs_2_, ...), custom_call_target="tpu_custom_call" | custom-call | flops 272629760 | bytes 1597440 | tf_op jit(solution)/shard_map/pallas_call | solution.py:167
  19.1 1.6 %collective-permute-start.6 = (f32[2,128]{1,0:T(2,128)S(1)}, f32[2,128]{1,0:T(2,128)S(1)}, u32[]{:S(2)}, u32[]{:S(2)}) collective-permute-start(f32[2,128]{1,0:T(2,128)S(1)} %slice.13), channel_id=1, source_target_pairs={{0,2},{1,3},{2,0},{3,1},{4,6},{5,7},{6,4},{7,5},{8,10},{9,11},{10,... | collective-permute-start | bytes 3080 | tf_op jit(solution)/shard_map/ppermute | solution.py:148
  20.6 2.4 %collective-permute-start.5 = (f32[1,128]{1,0:T(1,128)S(1)}, f32[1,128]{1,0:T(1,128)S(1)}, u32[]{:S(2)}, u32[]{:S(2)}) collective-permute-start(f32[1,128]{1,0:T(1,128)S(1)} %bitcast.4), channel_id=1, source_target_pairs={{0,12},{8,0},{4,8},{12,4},{1,13},{9,1},{5,9},{13,5},{2,14},{10,2},... | collective-permute-start | bytes 1544 | tf_op jit(solution)/shard_map/ppermute | solution.py:145
  23.1 0.0 collective-permute-done.6
  23.1 0.1 collective-permute-start.7
  23.1 0.5 %shard_map.29 = f32[1,128]{1,0:T(1,128)S(1)} custom-call(bf16[1040,128]{1,0:T(8,128)(2,1)S(1)} %collective-permute-done.refs_0_, bf16[1040,128]{1,0:T(8,128)(2,1)S(1)} %collective-permute-done.1.refs_1_, bf16[1040,128]{1,0:T(8,128)(2,1)S(1)} %collective-permute-done.2.refs_2_, bf16[1040,128]{1,0:T(8,128)(2,1)S(1)} %collective-permute-done.3.refs_3_, ...), custom_call_target="tpu_custom_call" | custom-call | flops 136314880 | bytes 1331200 | tf_op jit(solution)/shard_map/pallas_call | solution.py:176
  23.7 1.4 %collective-permute-done.5 = f32[1,128]{1,0:T(1,128)S(1)} collective-permute-done((f32[1,128]{1,0:T(1,128)S(1)}, f32[1,128]{1,0:T(1,128)S(1)}, u32[]{:S(2)}, u32[]{:S(2)}) %collective-permute-start.5) | collective-permute-done | bytes 544 | tf_op jit(solution)/shard_map/ppermute | solution.py:145
  25.1 0.0 collective-permute-done.7
  25.1 0.5 %maximum_bitcast_fusion = f32[128]{0:T(128)} fusion(f32[1,128]{1,0:T(1,128)S(1)} %collective-permute-done.7, f32[2,128]{1,0:T(2,128)S(1)} %slice_maximum_fusion, f32[1,128]{1,0:T(1,128)S(1)} %shard_map.29, f32[1,128]{1,0:T(1,128)S(1)} %collective-permute-done.5), kind=kLoop, calls=%fused_computation.1 | loop fusion | flops 384 | bytes 2560 | tf_op jit(solution)/shard_map/reshape | solution.py:189
  (3 shorter events, 0.0 us)
Async XLA Ops:
  1.2 12.4 %collective-permute-start.4 = (bf16[1040,128]{1,0:T(8,128)(2,1)S(1)}, bf16[1040,128]{1,0:T(8,128)(2,1)S(1)}, u32[]{:S(2)}, u32[]{:S(2)}) collective-permute-start(bf16[1040,128]{1,0:T(8,128)(2,1)S(1)} %shard_map.28.refs_5_), channel_id=1, source_target_pairs={{0,8},{8,4},{4,12},{12,0},{1,9},{9,5},{5,13},{13,1},{2,10},{10,6},... | collective-permute-start | bytes 798728 | tf_op jit(solution)/shard_map/ppermute | solution.py:145
  5.3 9.3 %collective-permute-start.3 = (bf16[1040,128]{1,0:T(8,128)(2,1)S(1)}, bf16[1040,128]{1,0:T(8,128)(2,1)S(1)}, u32[]{:S(2)}, u32[]{:S(2)}) collective-permute-start(bf16[1040,128]{1,0:T(8,128)(2,1)S(1)} %shard_map.28.refs_5_), channel_id=1, source_target_pairs={{0,2},{1,3},{2,0},{3,1},{4,6},{5,7},{6,4},{7,5},{8,10},{9,11},{10,... | collective-permute-start | bytes 798728 | tf_op jit(solution)/shard_map/ppermute | solution.py:148
  6.8 11.7 %collective-permute-start.2 = (bf16[1040,128]{1,0:T(8,128)(2,1)S(1)}, bf16[1040,128]{1,0:T(8,128)(2,1)S(1)}, u32[]{:S(2)}, u32[]{:S(2)}) collective-permute-start(bf16[1040,128]{1,0:T(8,128)(2,1)S(1)} %shard_map.28.refs_5_), channel_id=1, source_target_pairs={{0,4},{8,12},{4,0},{12,8},{1,5},{9,13},{5,1},{13,9},{2,6},{10,14},... | collective-permute-start | bytes 798728 | tf_op jit(solution)/shard_map/ppermute | solution.py:145
  8.4 10.1 %collective-permute-start.1 = (bf16[1040,128]{1,0:T(8,128)(2,1)S(1)}, bf16[1040,128]{1,0:T(8,128)(2,1)S(1)}, u32[]{:S(2)}, u32[]{:S(2)}) collective-permute-start(bf16[1040,128]{1,0:T(8,128)(2,1)S(1)} %shard_map.28.refs_5_), channel_id=1, source_target_pairs={{0,3},{1,2},{2,1},{3,0},{4,7},{5,6},{6,5},{7,4},{8,11},{9,10},{10,... | collective-permute-start | bytes 798728 | tf_op jit(solution)/shard_map/ppermute | solution.py:148
  8.4 10.1 %collective-permute-start = (bf16[1040,128]{1,0:T(8,128)(2,1)S(1)}, bf16[1040,128]{1,0:T(8,128)(2,1)S(1)}, u32[]{:S(2)}, u32[]{:S(2)}) collective-permute-start(bf16[1040,128]{1,0:T(8,128)(2,1)S(1)} %shard_map.28.refs_5_), channel_id=1, source_target_pairs={{0,1},{1,0},{2,3},{3,2},{4,5},{5,4},{6,7},{7,6},{8,9},{9,8},{10,11... | collective-permute-start | bytes 798728 | tf_op jit(solution)/shard_map/ppermute | solution.py:148
  19.1 4.0 %collective-permute-start.6 = (f32[2,128]{1,0:T(2,128)S(1)}, f32[2,128]{1,0:T(2,128)S(1)}, u32[]{:S(2)}, u32[]{:S(2)}) collective-permute-start(f32[2,128]{1,0:T(2,128)S(1)} %slice.13), channel_id=1, source_target_pairs={{0,2},{1,3},{2,0},{3,1},{4,6},{5,7},{6,4},{7,5},{8,10},{9,11},{10,... | collective-permute-start | bytes 3080 | tf_op jit(solution)/shard_map/ppermute | solution.py:148
  20.6 4.4 %collective-permute-start.5 = (f32[1,128]{1,0:T(1,128)S(1)}, f32[1,128]{1,0:T(1,128)S(1)}, u32[]{:S(2)}, u32[]{:S(2)}) collective-permute-start(f32[1,128]{1,0:T(1,128)S(1)} %bitcast.4), channel_id=1, source_target_pairs={{0,12},{8,0},{4,8},{12,4},{1,13},{9,1},{5,9},{13,5},{2,14},{10,2},... | collective-permute-start | bytes 1544 | tf_op jit(solution)/shard_map/ppermute | solution.py:145
  23.1 2.0 %collective-permute-start.7 = (f32[1,128]{1,0:T(1,128)S(1)}, f32[1,128]{1,0:T(1,128)S(1)}, u32[]{:S(2)}, u32[]{:S(2)}) collective-permute-start(f32[1,128]{1,0:T(1,128)S(1)} %slice.15), channel_id=1, source_target_pairs={{0,1},{1,0},{2,3},{3,2},{4,5},{5,4},{6,7},{7,6},{8,9},{9,8},{10,11... | collective-permute-start | bytes 1544 | tf_op jit(solution)/shard_map/ppermute | solution.py:148

commit v5 on v4

--- a/solution.py
+++ b/solution.py
@@ -110,16 +110,25 @@
     refs[-1][...] = row_maxima(masked_scores(column[:1], column, rows, True)[0])
 
 
-def moved_kernel(*refs, rows, place):
+def moved_kernel(*refs, rows, place, last):
     left = [refs[i] for i in place["left"]]
     column = [refs[i] for i in place["column"]]
     turn_ref, part_ref = refs[-2:]
     masked = masked_scores(left, column, rows, False)
-    for t in range(turn_ref.shape[0]):
+    for t in range(len(left)):
         turn_ref[t] = row_maxima(masked[t])
+    parts = []
     for k in range(len(column)):
         part = functools.reduce(jnp.maximum, [masked[t][k] for t in range(len(left))])
-        part_ref[pl.ds(k, 1), :] = jnp.max(part, axis=0, keepdims=True)
+        parts.append(jnp.max(part, axis=0, keepdims=True))
+    if last:
+        here = lax.axis_index("dev") == last
+        parts[1], parts[2] = (
+            jnp.where(here, parts[2], parts[1]),
+            jnp.where(here, parts[1], parts[2]),
+        )
+    for k, part in enumerate(parts):
+        part_ref[pl.ds(k, 1), :] = part
 
 
 def cost(lefts, column):
@@ -140,23 +149,36 @@
     columns, lanes = lax.axis_size("dev"), lax.axis_size("sub")
     order = column_order(columns)
 
-    def along_dev(value, step):
-        pairs = [(order[i], order[(i + step) % columns]) for i in range(columns)]
-        return lax.ppermute(value, "dev", pairs)
+    def along_dev(value, steps):
+        pairs = [
+            (order[i] * lanes + k, order[(i + steps[k % 2]) % columns] * lanes + k)
+            for i in range(columns)
+            for k in range(lanes)
+        ]
+        return lax.ppermute(value, ("dev", "sub"), pairs)
 
     def along_sub(value, flip):
         return lax.ppermute(value, "sub", [(i, i ^ flip) for i in range(lanes)])
 
+    last = columns - 1 if lanes == 4 else 0
+
+    def by_column(value, flip, last_flip):
+        pairs = [
+            (i * lanes + k, i * lanes + (k ^ (last_flip if i == last else flip)))
+            for i in range(columns)
+            for k in range(lanes)
+        ]
+        return lax.ppermute(value, ("dev", "sub"), pairs)
+
     own = pack(embeds, assignment)
-    turns = list(range(1, (columns + 1) // 2))
-    left = [along_dev(own, step) for step in turns]
-    if columns % 2 == 0:
-        left.append(along_dev(own, columns // 2))
+    steps = list(range(1, columns // 2 + 1))
+    turns = steps[: (columns - 1) // 2]
+    left = [along_dev(own, pair) for pair in zip(steps, steps[::-1])]
     column = [own] + [along_sub(own, flip) for flip in range(1, lanes)]
 
     named = [(("left", t), value) for t, value in enumerate(left)]
     named += [(("column", k), value) for k, value in enumerate(column)]
-    first = [('left', 0), ('column', 2), ('left', 1), ('column', 3), ('column', 1)]
+    first = [('left', 0), ('column', 2), ('column', 3), ('left', 1), ('column', 1)]
     named.sort(key=lambda item: -first.index(item[0]) if item[0] in first else 1)
     blocks = [value for _, value in named]
     names = [name for name, _ in named]
@@ -165,9 +187,9 @@
         "column": [names.index(("column", k)) for k in range(lanes)],
     }
     turn_best, part = pl.pallas_call(
-        functools.partial(moved_kernel, rows=rows, place=place),
+        functools.partial(moved_kernel, rows=rows, place=place, last=last),
         out_shape=[
-            jax.ShapeDtypeStruct((len(turns), 1, rows), jnp.float32),
+            jax.ShapeDtypeStruct((len(left), 1, rows), jnp.float32),
             jax.ShapeDtypeStruct((lanes, rows), jnp.float32),
         ],
         cost_estimate=cost(len(left), column),
@@ -180,12 +202,20 @@
         compiler_params=pltpu.CompilerParams(vmem_limit_bytes=VMEM_BYTES),
     )(*blocks)
 
-    best = [own_best] + [along_dev(turn_best[t], -step) for t, step in enumerate(turns)]
-    pair = part[:2]
-    for flip in range(2, lanes, 2):
-        pair = jnp.maximum(pair, along_sub(part[flip : flip + 2], flip))
+    odd = lax.axis_index("sub") % 2 == 1
+    best = [own_best]
+    for t, step in enumerate(turns):
+        back = jnp.where(odd, turn_best[len(steps) - 1 - t], turn_best[t])
+        best.append(along_dev(back, (-step, -step)))
+    if last:
+        pair = jnp.maximum(part[:2], by_column(part[2:], 2, 1))
+        best.append(by_column(pair[1:], 1, 2))
+    else:
+        pair = part[:2]
+        for flip in range(2, lanes, 2):
+            pair = jnp.maximum(pair, along_sub(part[flip : flip + 2], flip))
+        best.append(along_sub(pair[1:], 1))
     best.append(pair[:1])
-    best.append(along_sub(pair[1:], 1))
     return functools.reduce(jnp.maximum, best).reshape(rows)
 
 

time: 25.7 us -> 24.6 us (0.957)
  waiting for transfers between devices: 10.9 us -> 9.63 us
    ppermute x3 -> x5, waiting for transfers between devices: 9.86 us -> 6.41 us  [the longest x3 6.4 us: along_dev(): return lax.ppermute(value, ('dev', 'sub'), pairs)]
    ppermute x3 -> x5, starting transfers between devices: 8.1 us -> 10.4 us  [the longest x3 9.27 us: along_dev(): return lax.ppermute(value, ('dev', 'sub'), pairs)]
    ppermute x5 -> x3, starting transfers between devices: 3.77 us -> 1.5 us  [along_sub(): return lax.ppermute(value, 'sub', [(i, i ^ flip) for i in range(lanes)])]
    ppermute x5 -> x3, waiting for transfers between devices: 1 us -> 3.23 us  [along_sub(): return lax.ppermute(value, 'sub', [(i, i ^ flip) for i in range(lanes)])]
  transfers between devices with their start and end apart: 8 -> 8, of which waited for: 4 -> 5; matrix products, arithmetic and copies ran while one was open for 0% -> 0% of each run, Pallas kernels for 2% -> 2%
where the time goes in v5:
time: 24.6 us; the launch traced here: 24.4 us
  starting transfers between devices  11.9 us (48%)
  waiting for transfers between devices  9.63 us (39%)
  Pallas kernels  2.31 us (9%)
  other arithmetic  0.52 us (2%)
    ppermute x3, starting transfers between devices, along_dev(): return lax.ppermute(value, ('dev', 'sub'), pairs)  9.27 us
    ppermute x3, waiting for transfers between devices, along_dev(): return lax.ppermute(value, ('dev', 'sub'), pairs)  6.4 us
    ppermute x3, waiting for transfers between devices, along_sub(): return lax.ppermute(value, 'sub', [(i, i ^ flip) for i in range(lanes)])  3.23 us
    ppermute x3, starting transfers between devices, along_sub(): return lax.ppermute(value, 'sub', [(i, i ^ flip) for i in range(lanes)])  1.5 us
    pallas_call x1, Pallas kernels, pack(): pl.pallas_call(pack_kernel, out_shape=jax.ShapeDtypeStruct((width // LANE...  1.2 us
    ppermute x2, starting transfers between devices, by_column(): return lax.ppermute(value, ('dev', 'sub'), pairs)  1.16 us
    pallas_call x1, Pallas kernels, on_device(): pl.pallas_call(functools.partial(moved_kernel, rows=rows, place=place, la...  0.55 us
    pallas_call x1, Pallas kernels, on_device(): pl.pallas_call(functools.partial(own_kernel, rows=rows, place=place), out...  0.55 us
  transfers between devices with their start and end apart: 8, of which 5 were waited for; matrix products, arithmetic and copies ran while one was open for 0% of the time, Pallas kernels for 2%

profile of v5, /device:TPU:0, one launch (start us, length us, event | category | flops | bytes accessed | tf_op | source)
XLA Modules:
  0.0 24.4 jit_solution(12465884723430706490)
XLA Ops:
  0.0 1.2 %shard_map.28.refs_5_ = bf16[1040,128]{1,0:T(8,128)(2,1)S(1)} custom-call(f32[128,1024]{1,0:T(8,128)} %embeds_hbm.1, s32[1,128]{1,0:T(1,128)} %bitcast.5), custom_call_target="tpu_custom_call" | custom-call | tf_op jit(solution)/shard_map/pallas_call | solution.py:54
  1.2 4.1 %collective-permute-start.4 = (bf16[1040,128]{1,0:T(8,128)(2,1)S(1)}, bf16[1040,128]{1,0:T(8,128)(2,1)S(1)}, u32[]{:S(2)}, u32[]{:S(2)}) collective-permute-start(bf16[1040,128]{1,0:T(8,128)(2,1)S(1)} %shard_map.28.refs_5_), channel_id=1, source_target_pairs={{0,8},{1,5},{2,10},{3,7},{8,4},{9,13},{10,6},{11,15},{4,12},{5,1},... | collective-permute-start | bytes 798728 | tf_op jit(solution)/shard_map/ppermute | solution.py:158
  5.3 1.5 %collective-permute-start.3 = (bf16[1040,128]{1,0:T(8,128)(2,1)S(1)}, bf16[1040,128]{1,0:T(8,128)(2,1)S(1)}, u32[]{:S(2)}, u32[]{:S(2)}) collective-permute-start(bf16[1040,128]{1,0:T(8,128)(2,1)S(1)} %shard_map.28.refs_5_), channel_id=1, source_target_pairs={{0,2},{1,3},{2,0},{3,1},{4,6},{5,7},{6,4},{7,5},{8,10},{9,11},{10,... | collective-permute-start | bytes 798728 | tf_op jit(solution)/shard_map/ppermute | solution.py:161
  6.8 0.0 collective-permute-start.2
  6.8 1.6 %collective-permute-start.1 = (bf16[1040,128]{1,0:T(8,128)(2,1)S(1)}, bf16[1040,128]{1,0:T(8,128)(2,1)S(1)}, u32[]{:S(2)}, u32[]{:S(2)}) collective-permute-start(bf16[1040,128]{1,0:T(8,128)(2,1)S(1)} %shard_map.28.refs_5_), channel_id=1, source_target_pairs={{0,4},{1,9},{2,6},{3,11},{8,12},{9,5},{10,14},{11,7},{4,0},{5,13},... | collective-permute-start | bytes 798728 | tf_op jit(solution)/shard_map/ppermute | solution.py:158
  8.4 0.0 collective-permute-start
  8.4 5.3 %collective-permute-done.4.refs_4_ = bf16[1040,128]{1,0:T(8,128)(2,1)S(1)} collective-permute-done((bf16[1040,128]{1,0:T(8,128)(2,1)S(1)}, bf16[1040,128]{1,0:T(8,128)(2,1)S(1)}, u32[]{:S(2)}, u32[]{:S(2)}) %collective-permute-start.4) | collective-permute-done | bytes 266272 | tf_op jit(solution)/shard_map/ppermute | solution.py:158
  13.6 0.9 %collective-permute-done.3.refs_3_ = bf16[1040,128]{1,0:T(8,128)(2,1)S(1)} collective-permute-done((bf16[1040,128]{1,0:T(8,128)(2,1)S(1)}, bf16[1040,128]{1,0:T(8,128)(2,1)S(1)}, u32[]{:S(2)}, u32[]{:S(2)}) %collective-permute-start.3) | collective-permute-done | bytes 266272 | tf_op jit(solution)/shard_map/ppermute | solution.py:161
  14.5 2.3 %collective-permute-done.2.refs_2_ = bf16[1040,128]{1,0:T(8,128)(2,1)S(1)} collective-permute-done((bf16[1040,128]{1,0:T(8,128)(2,1)S(1)}, bf16[1040,128]{1,0:T(8,128)(2,1)S(1)}, u32[]{:S(2)}, u32[]{:S(2)}) %collective-permute-start.2) | collective-permute-done | bytes 266272 | tf_op jit(solution)/shard_map/ppermute | solution.py:161
  16.9 0.5 %collective-permute-done.1.refs_1_ = bf16[1040,128]{1,0:T(8,128)(2,1)S(1)} collective-permute-done((bf16[1040,128]{1,0:T(8,128)(2,1)S(1)}, bf16[1040,128]{1,0:T(8,128)(2,1)S(1)}, u32[]{:S(2)}, u32[]{:S(2)}) %collective-permute-start.1) | collective-permute-done | bytes 266272 | tf_op jit(solution)/shard_map/ppermute | solution.py:158
  17.4 0.0 collective-permute-done.refs_0_
  17.4 0.6 %shard_map.30 = (f32[2,1,128]{2,1,0:T(1,128)S(1)}, f32[4,128]{1,0:T(4,128)S(1)}) custom-call(bf16[1040,128]{1,0:T(8,128)(2,1)S(1)} %collective-permute-done.refs_0_, bf16[1040,128]{1,0:T(8,128)(2,1)S(1)} %collective-permute-done.1.refs_1_, bf16[1040,128]{1,0:T(8,128)(2,1)S(1)} %collective-permute-done.2.refs_2_, ...), custom_call_target="tpu_custom_call" | custom-call | flops 272629760 | bytes 1597440 | tf_op jit(solution)/shard_map/pallas_call | solution.py:189
  17.9 1.1 %collective-permute-start.6 = (f32[2,128]{1,0:T(2,128)S(1)}, f32[2,128]{1,0:T(2,128)S(1)}, u32[]{:S(2)}, u32[]{:S(2)}) collective-permute-start(f32[2,128]{1,0:T(2,128)S(1)} %slice.21), channel_id=1, source_target_pairs={{0,2},{1,3},{2,0},{3,1},{4,6},{5,7},{6,4},{7,5},{8,10},{9,11},{10,... | collective-permute-start | bytes 3080 | tf_op jit(solution)/shard_map/ppermute | solution.py:171
  19.0 3.6 %collective-permute-start.5 = (f32[1,128]{1,0:T(1,128)S(1)}, f32[1,128]{1,0:T(1,128)S(1)}, u32[]{:S(2)}, u32[]{:S(2)}) collective-permute-start(f32[1,128]{1,0:T(1,128)S(1)} %fusion), channel_id=1, source_target_pairs={{0,12},{1,13},{2,14},{3,15},{8,0},{9,1},{10,2},{11,3},{4,8},{5,9},... | collective-permute-start | bytes 1544 | tf_op jit(solution)/shard_map/ppermute | solution.py:158
  22.6 0.0 collective-permute-done.6
  22.6 0.1 collective-permute-start.7
  22.7 0.6 %shard_map.29 = f32[1,128]{1,0:T(1,128)S(1)} custom-call(bf16[1040,128]{1,0:T(8,128)(2,1)S(1)} %collective-permute-done.refs_0_, bf16[1040,128]{1,0:T(8,128)(2,1)S(1)} %collective-permute-done.1.refs_1_, bf16[1040,128]{1,0:T(8,128)(2,1)S(1)} %collective-permute-done.2.refs_2_, bf16[1040,128]{1,0:T(8,128)(2,1)S(1)} %collective-permute-done.3.refs_3_, ...), custom_call_target="tpu_custom_call" | custom-call | flops 136314880 | bytes 1331200 | tf_op jit(solution)/shard_map/pallas_call | solution.py:198
  23.3 0.6 %collective-permute-done.5 = f32[1,128]{1,0:T(1,128)S(1)} collective-permute-done((f32[1,128]{1,0:T(1,128)S(1)}, f32[1,128]{1,0:T(1,128)S(1)}, u32[]{:S(2)}, u32[]{:S(2)}) %collective-permute-start.5) | collective-permute-done | bytes 544 | tf_op jit(solution)/shard_map/ppermute | solution.py:158
  23.9 0.0 collective-permute-done.7
  23.9 0.5 %maximum_bitcast_fusion = f32[128]{0:T(128)} fusion(f32[2,128]{1,0:T(2,128)S(1)} %slice_maximum_fusion, f32[1,128]{1,0:T(1,128)S(1)} %collective-permute-done.7, f32[1,128]{1,0:T(1,128)S(1)} %shard_map.29, f32[1,128]{1,0:T(1,128)S(1)} %collective-permute-done.5), kind=kLoop, calls=%fused_computation.3 | loop fusion | flops 384 | bytes 2560 | tf_op jit(solution)/shard_map/reshape | solution.py:219
  (4 shorter events, 0.0 us)
Async XLA Ops:
  1.2 12.4 %collective-permute-start.4 = (bf16[1040,128]{1,0:T(8,128)(2,1)S(1)}, bf16[1040,128]{1,0:T(8,128)(2,1)S(1)}, u32[]{:S(2)}, u32[]{:S(2)}) collective-permute-start(bf16[1040,128]{1,0:T(8,128)(2,1)S(1)} %shard_map.28.refs_5_), channel_id=1, source_target_pairs={{0,8},{1,5},{2,10},{3,7},{8,4},{9,13},{10,6},{11,15},{4,12},{5,1},... | collective-permute-start | bytes 798728 | tf_op jit(solution)/shard_map/ppermute | solution.py:158
  5.3 9.2 %collective-permute-start.3 = (bf16[1040,128]{1,0:T(8,128)(2,1)S(1)}, bf16[1040,128]{1,0:T(8,128)(2,1)S(1)}, u32[]{:S(2)}, u32[]{:S(2)}) collective-permute-start(bf16[1040,128]{1,0:T(8,128)(2,1)S(1)} %shard_map.28.refs_5_), channel_id=1, source_target_pairs={{0,2},{1,3},{2,0},{3,1},{4,6},{5,7},{6,4},{7,5},{8,10},{9,11},{10,... | collective-permute-start | bytes 798728 | tf_op jit(solution)/shard_map/ppermute | solution.py:161
  6.8 10.1 %collective-permute-start.2 = (bf16[1040,128]{1,0:T(8,128)(2,1)S(1)}, bf16[1040,128]{1,0:T(8,128)(2,1)S(1)}, u32[]{:S(2)}, u32[]{:S(2)}) collective-permute-start(bf16[1040,128]{1,0:T(8,128)(2,1)S(1)} %shard_map.28.refs_5_), channel_id=1, source_target_pairs={{0,3},{1,2},{2,1},{3,0},{4,7},{5,6},{6,5},{7,4},{8,11},{9,10},{10,... | collective-permute-start | bytes 798728 | tf_op jit(solution)/shard_map/ppermute | solution.py:161
  6.8 10.6 %collective-permute-start.1 = (bf16[1040,128]{1,0:T(8,128)(2,1)S(1)}, bf16[1040,128]{1,0:T(8,128)(2,1)S(1)}, u32[]{:S(2)}, u32[]{:S(2)}) collective-permute-start(bf16[1040,128]{1,0:T(8,128)(2,1)S(1)} %shard_map.28.refs_5_), channel_id=1, source_target_pairs={{0,4},{1,9},{2,6},{3,11},{8,12},{9,5},{10,14},{11,7},{4,0},{5,13},... | collective-permute-start | bytes 798728 | tf_op jit(solution)/shard_map/ppermute | solution.py:158
  8.4 9.0 %collective-permute-start = (bf16[1040,128]{1,0:T(8,128)(2,1)S(1)}, bf16[1040,128]{1,0:T(8,128)(2,1)S(1)}, u32[]{:S(2)}, u32[]{:S(2)}) collective-permute-start(bf16[1040,128]{1,0:T(8,128)(2,1)S(1)} %shard_map.28.refs_5_), channel_id=1, source_target_pairs={{0,1},{1,0},{2,3},{3,2},{4,5},{5,4},{6,7},{7,6},{8,9},{9,8},{10,11... | collective-permute-start | bytes 798728 | tf_op jit(solution)/shard_map/ppermute | solution.py:161
  17.9 4.7 %collective-permute-start.6 = (f32[2,128]{1,0:T(2,128)S(1)}, f32[2,128]{1,0:T(2,128)S(1)}, u32[]{:S(2)}, u32[]{:S(2)}) collective-permute-start(f32[2,128]{1,0:T(2,128)S(1)} %slice.21), channel_id=1, source_target_pairs={{0,2},{1,3},{2,0},{3,1},{4,6},{5,7},{6,4},{7,5},{8,10},{9,11},{10,... | collective-permute-start | bytes 3080 | tf_op jit(solution)/shard_map/ppermute | solution.py:171
  19.0 4.9 %collective-permute-start.5 = (f32[1,128]{1,0:T(1,128)S(1)}, f32[1,128]{1,0:T(1,128)S(1)}, u32[]{:S(2)}, u32[]{:S(2)}) collective-permute-start(f32[1,128]{1,0:T(1,128)S(1)} %fusion), channel_id=1, source_target_pairs={{0,12},{1,13},{2,14},{3,15},{8,0},{9,1},{10,2},{11,3},{4,8},{5,9},... | collective-permute-start | bytes 1544 | tf_op jit(solution)/shard_map/ppermute | solution.py:158
  22.6 1.3 %collective-permute-start.7 = (f32[1,128]{1,0:T(1,128)S(1)}, f32[1,128]{1,0:T(1,128)S(1)}, u32[]{:S(2)}, u32[]{:S(2)}) collective-permute-start(f32[1,128]{1,0:T(1,128)S(1)} %slice.22), channel_id=1, source_target_pairs={{0,1},{1,0},{2,3},{3,2},{4,5},{5,4},{6,7},{7,6},{8,9},{9,8},{10,11... | collective-permute-start | bytes 1544 | tf_op jit(solution)/shard_map/ppermute | solution.py:171

commit v6 on v5

--- a/solution.py
+++ b/solution.py
@@ -10,6 +10,7 @@
 LANES = 128
 ID_ROWS = 16
 LOWEST = -1.0
+ORDERS = (('turn', 'x', 'swap'), ('x', 'swap', 'turn'))
 CHUNKS = 1
 VMEM_BYTES = 16 * 1024 * 1024
 
@@ -26,9 +27,9 @@
         for c in range(CHUNKS)
     ]
     copy_ids = pltpu.make_async_copy(ids_hbm, ids_ref, ids_sem)
-    copy_ids.start()
     for copy in copies:
         copy.start()
+    copy_ids.start()
     copy_ids.wait()
     ids = ids_ref[...].astype(jnp.float32)
     out_ref[pl.ds(width // LANES * rows, ID_ROWS), :] = jnp.broadcast_to(
@@ -65,38 +66,36 @@
     )(*operands)
 
 
-def load_rows(ref, rows):
-    blocks = (ref.shape[0] - ID_ROWS) // rows
-    return jnp.concatenate([ref[pl.ds(b * rows, rows), :] for b in range(blocks)], axis=1)
-
-
-def load_ids(ref):
+def load(ref):
     start = ref.shape[0] - ID_ROWS
-    return ref[pl.ds(start, ID_ROWS), :].astype(jnp.float32)[:1, :]
-
-
-def masked_scores(left_refs, column_refs, rows, own):
-    left = jnp.concatenate([load_rows(ref, rows) for ref in left_refs], axis=0)
-    left_ids = [jnp.broadcast_to(load_ids(ref), (rows, rows)).T for ref in left_refs]
-    masked = [[] for _ in left_refs]
-    for start in range(0, len(column_refs), 4):
-        refs = column_refs[start : start + 4]
-        scores = lax.dot_general(
-            left,
-            jnp.concatenate([load_rows(ref, rows) for ref in refs], axis=0),
-            (((1,), (1,)), ((), ())),
-            preferred_element_type=jnp.float32,
-        )
-        for j, ref in enumerate(refs):
-            ids = load_ids(ref)
-            for t in range(len(left_refs)):
-                same = left_ids[t] == ids
-                if own and start + j == 0:
-                    down = lax.broadcasted_iota(jnp.int32, (rows, rows), 0)
-                    across = lax.broadcasted_iota(jnp.int32, (rows, rows), 1)
-                    same = same & (down != across)
-                part = scores[t * rows : (t + 1) * rows, j * rows : (j + 1) * rows]
-                masked[t].append(jnp.where(same, part, jnp.float32(LOWEST)))
+    parts = [ref[pl.ds(b * LANES, LANES), :] for b in range(start // LANES)]
+    return jnp.concatenate(parts, axis=1), ref[pl.ds(start, ID_ROWS), :]
+
+
+def choose(here, one, other):
+    return jax.tree.map(lambda a, b: jnp.where(here, a, b), one, other)
+
+
+def masked_scores(left, column, rows, own):
+    line = [ids.astype(jnp.float32)[:1, :] for _, ids in column]
+    scores = lax.dot_general(
+        jnp.concatenate([value for value, _ in left], axis=0),
+        jnp.concatenate([value for value, _ in column], axis=0),
+        (((1,), (1,)), ((), ())),
+        preferred_element_type=jnp.float32,
+    )
+    masked = []
+    for t, (_, ids) in enumerate(left):
+        left_ids = jnp.broadcast_to(ids.astype(jnp.float32)[:1, :], (rows, rows)).T
+        masked.append([])
+        for k in range(len(column)):
+            same = left_ids == line[k]
+            if own and k == 0:
+                down = lax.broadcasted_iota(jnp.int32, (rows, rows), 0)
+                across = lax.broadcasted_iota(jnp.int32, (rows, rows), 1)
+                same = same & (down != across)
+            part = scores[t * rows : (t + 1) * rows, k * rows : (k + 1) * rows]
+            masked[t].append(jnp.where(same, part, jnp.float32(LOWEST)))
     return masked
 
 
@@ -105,18 +104,51 @@
     return jnp.max(best.T, axis=0, keepdims=True)
 
 
+def unpack(refs, place):
+    left = [load(refs[i]) for i in place["left"]]
+    column = [load(refs[i]) for i in place["column"]]
+    if len(left) == 3:
+        odd = lax.rem(lax.axis_index("sub"), 2) == 1
+        even_x, odd_x = (moves.index("x") for moves in ORDERS)
+        column.insert(2, choose(odd, left[odd_x], left[even_x]))
+        if even_x != odd_x:
+            left[even_x] = choose(odd, left[even_x], left[odd_x])
+        del left[odd_x]
+    return left, column
+
+
 def own_kernel(*refs, rows, place):
-    column = [refs[i] for i in place["column"]]
+    _, column = unpack(refs[:-1], place)
     refs[-1][...] = row_maxima(masked_scores(column[:1], column, rows, True)[0])
 
 
-def moved_kernel(*refs, rows, place, last):
-    left = [refs[i] for i in place["left"]]
-    column = [refs[i] for i in place["column"]]
-    turn_ref, part_ref = refs[-2:]
+def rotation_places():
+    even_x, odd_x = (moves.index("x") for moves in ORDERS)
+    even = [move for i, move in enumerate(ORDERS[0])]
+    odd = [move for i, move in enumerate(ORDERS[1])]
+    if even_x != odd_x:
+        even[even_x] = even[odd_x]
+        odd[even_x] = odd[even_x]
+    del even[odd_x], odd[odd_x]
+    return even.index("turn"), odd.index("turn")
+
+
+def moved_kernel(*refs, rows, place, turns, last):
+    left, column = unpack(refs, place)
+    *turn_refs, pass_ref, keep_ref = refs[-2 - max(turns, 1) :]
     masked = masked_scores(left, column, rows, False)
-    for t in range(len(left)):
-        turn_ref[t] = row_maxima(masked[t])
+    odd = lax.rem(lax.axis_index("sub"), 2) == 1
+    for t in range(turns):
+        best = functools.reduce(jnp.maximum, masked[t])
+        if last:
+            even_turn, odd_turn = rotation_places()
+            best = functools.reduce(jnp.maximum, masked[even_turn])
+            other = functools.reduce(jnp.maximum, masked[odd_turn])
+            best = jnp.where(odd, other, best)
+        elif len(left) > 1:
+            other = functools.reduce(jnp.maximum, masked[-1 - t])
+            best = jnp.where(odd, other, best)
+        turn_refs[t][...] = jnp.max(best.T, axis=0, keepdims=True)
     parts = []
     for k in range(len(column)):
         part = functools.reduce(jnp.maximum, [masked[t][k] for t in range(len(left))])
@@ -128,7 +160,8 @@
             jnp.where(here, parts[1], parts[2]),
         )
     for k, part in enumerate(parts):
-        part_ref[pl.ds(k, 1), :] = part
+        ref, row = (keep_ref, k) if k < 2 else (pass_ref, k - 2)
+        ref[pl.ds(row, 1), :] = part
 
 
 def cost(lefts, column):
@@ -160,7 +193,7 @@
     def along_sub(value, flip):
         return lax.ppermute(value, "sub", [(i, i ^ flip) for i in range(lanes)])
 
-    last = columns - 1 if lanes == 4 else 0
+    last = columns - 1 if lanes == 4 and columns == 4 else 0
 
     def by_column(value, flip, last_flip):
         pairs = [
@@ -173,26 +206,41 @@
     own = pack(embeds, assignment)
     steps = list(range(1, columns // 2 + 1))
     turns = steps[: (columns - 1) // 2]
-    left = [along_dev(own, pair) for pair in zip(steps, steps[::-1])]
-    column = [own] + [along_sub(own, flip) for flip in range(1, lanes)]
+    if last:
+        left = []
+        for moves in zip(*ORDERS):
+            pairs = []
+            for i in range(columns):
+                for k in range(lanes):
+                    move = moves[k % 2]
+                    step = {"turn": 1, "swap": 2, "x": 0}[move]
+                    j = order[(order.index(i) + step) % columns]
+                    pairs.append((i * lanes + k, j * lanes + (k ^ 2 if move == "x" else k)))
+            left.append(lax.ppermute(own, ("dev", "sub"), pairs))
+        column = [own, along_sub(own, 1), along_sub(own, 3)]
+    else:
+        left = [along_dev(own, pair) for pair in zip(steps, steps[::-1])]
+        column = [own] + [along_sub(own, flip) for flip in range(1, lanes)]
 
     named = [(("left", t), value) for t, value in enumerate(left)]
     named += [(("column", k), value) for k, value in enumerate(column)]
-    first = [('left', 0), ('column', 2), ('column', 3), ('left', 1), ('column', 1)]
+    first = [('left', 0), ('left', 1), ('column', 1), ('left', 2), ('column', 2)]
     named.sort(key=lambda item: -first.index(item[0]) if item[0] in first else 1)
     blocks = [value for _, value in named]
     names = [name for name, _ in named]
     place = {
         "left": [names.index(("left", t)) for t in range(len(left))],
-        "column": [names.index(("column", k)) for k in range(lanes)],
+        "column": [names.index(("column", k)) for k in range(len(column))],
     }
-    turn_best, part = pl.pallas_call(
-        functools.partial(moved_kernel, rows=rows, place=place, last=last),
-        out_shape=[
-            jax.ShapeDtypeStruct((len(left), 1, rows), jnp.float32),
-            jax.ShapeDtypeStruct((lanes, rows), jnp.float32),
+    line = jax.ShapeDtypeStruct((1, rows), jnp.float32)
+    *back, passed, kept = pl.pallas_call(
+        functools.partial(moved_kernel, rows=rows, place=place, turns=len(turns), last=last),
+        out_shape=[line] * max(len(turns), 1)
+        + [
+            jax.ShapeDtypeStruct((max(lanes - 2, 1), rows), jnp.float32),
+            jax.ShapeDtypeStruct((2, rows), jnp.float32),
         ],
-        cost_estimate=cost(len(left), column),
+        cost_estimate=cost(2, column),
         compiler_params=pltpu.CompilerParams(vmem_limit_bytes=VMEM_BYTES),
     )(*blocks)
     own_best = pl.pallas_call(
@@ -202,18 +250,16 @@
         compiler_params=pltpu.CompilerParams(vmem_limit_bytes=VMEM_BYTES),
     )(*blocks)
 
-    odd = lax.axis_index("sub") % 2 == 1
     best = [own_best]
-    for t, step in enumerate(turns):
-        back = jnp.where(odd, turn_best[len(steps) - 1 - t], turn_best[t])
-        best.append(along_dev(back, (-step, -step)))
+    for value, step in zip(back, turns):
+        best.append(along_dev(value, (-step, -step)))
     if last:
-        pair = jnp.maximum(part[:2], by_column(part[2:], 2, 1))
+        pair = jnp.maximum(kept, by_column(passed, 2, 1))
         best.append(by_column(pair[1:], 1, 2))
     else:
-        pair = part[:2]
+        pair = kept
         for flip in range(2, lanes, 2):
-            pair = jnp.maximum(pair, along_sub(part[flip : flip + 2], flip))
+            pair = jnp.maximum(pair, along_sub(passed[flip - 2 : flip], flip))
         best.append(along_sub(pair[1:], 1))
     best.append(pair[:1])
     return functools.reduce(jnp.maximum, best).reshape(rows)

time: 24.6 us -> 24.5 us (level)
    ppermute x0 -> x3, waiting for transfers between devices: none -> 8.52 us  [on_device(): left.append(lax.ppermute(own, ('dev', 'sub'), pairs))]
    ppermute x0 -> x3, starting transfers between devices: none -> 7.16 us  [on_device(): left.append(lax.ppermute(own, ('dev', 'sub'), pairs))]
    ppermute x3 -> x1, waiting for transfers between devices: 6.4 us -> 0.66 us  [along_dev(): return lax.ppermute(value, ('dev', 'sub'), pairs)]
    ppermute x3 -> x1, starting transfers between devices: 9.27 us -> 4.14 us  [along_dev(): return lax.ppermute(value, ('dev', 'sub'), pairs)]
    ppermute x3 -> x2, waiting for transfers between devices: 3.23 us -> 0.23 us  [along_sub(): return lax.ppermute(value, 'sub', [(i, i ^ flip) for i in range(lanes)])]
    ppermute x3 -> x2, starting transfers between devices: 1.5 us -> 0.01 us  [along_sub(): return lax.ppermute(value, 'sub', [(i, i ^ flip) for i in range(lanes)])]
    ppermute x2, starting transfers between devices: 1.16 us -> 0.81 us  [by_column(): return lax.ppermute(value, ('dev', 'sub'), pairs)]
  transfers between devices with their start and end apart: 8 -> 8, of which waited for: 5 -> 4; matrix products, arithmetic and copies ran while one was open for 0% -> 0% of each run, Pallas kernels for 2% -> 2%
where the time goes in v6:
time: 24.5 us; the launch traced here: 24.4 us
  starting transfers between devices  12.1 us (49%)
  waiting for transfers between devices  9.42 us (38%)
  Pallas kernels  2.27 us (9%)
  other arithmetic  0.52 us (2%)
    ppermute x3, waiting for transfers between devices, on_device(): left.append(lax.ppermute(own, ('dev', 'sub'), pairs))  8.52 us
    ppermute x3, starting transfers between devices, on_device(): left.append(lax.ppermute(own, ('dev', 'sub'), pairs))  7.16 us
    ppermute x1, starting transfers between devices, along_dev(): return lax.ppermute(value, ('dev', 'sub'), pairs)  4.14 us
    pallas_call x1, Pallas kernels, pack(): pl.pallas_call(pack_kernel, out_shape=jax.ShapeDtypeStruct((width // LANE...  1.18 us
    ppermute x2, starting transfers between devices, by_column(): return lax.ppermute(value, ('dev', 'sub'), pairs)  0.81 us
    ppermute x1, waiting for transfers between devices, along_dev(): return lax.ppermute(value, ('dev', 'sub'), pairs)  0.66 us
    pallas_call x1, Pallas kernels, on_device(): pl.pallas_call(functools.partial(moved_kernel, rows=rows, place=place, tu...  0.55 us
    pallas_call x1, Pallas kernels, on_device(): pl.pallas_call(functools.partial(own_kernel, rows=rows, place=place), out...  0.54 us
  transfers between devices with their start and end apart: 8, of which 4 were waited for; matrix products, arithmetic and copies ran while one was open for 0% of the time, Pallas kernels for 2%

profile of v6, /device:TPU:0, one launch (start us, length us, event | category | flops | bytes accessed | tf_op | source)
XLA Modules:
  0.0 24.4 jit_solution(6588818382754791982)
XLA Ops:
  0.0 1.2 %shard_map.28.refs_5_ = bf16[1040,128]{1,0:T(8,128)(2,1)S(1)} custom-call(f32[128,1024]{1,0:T(8,128)} %embeds_hbm.1, s32[1,128]{1,0:T(1,128)} %bitcast.3), custom_call_target="tpu_custom_call" | custom-call | tf_op jit(solution)/shard_map/pallas_call | solution.py:55
  1.2 4.1 %collective-permute-start.4 = (bf16[1040,128]{1,0:T(8,128)(2,1)S(1)}, bf16[1040,128]{1,0:T(8,128)(2,1)S(1)}, u32[]{:S(2)}, u32[]{:S(2)}) collective-permute-start(bf16[1040,128]{1,0:T(8,128)(2,1)S(1)} %shard_map.28.refs_5_), channel_id=1, source_target_pairs={{0,8},{1,3},{2,10},{3,1},{4,12},{5,7},{6,14},{7,5},{8,4},{9,11},{1... | collective-permute-start | bytes 798728 | tf_op jit(solution)/shard_map/ppermute | solution.py:219
  5.3 1.5 %collective-permute-start.3 = (bf16[1040,128]{1,0:T(8,128)(2,1)S(1)}, bf16[1040,128]{1,0:T(8,128)(2,1)S(1)}, u32[]{:S(2)}, u32[]{:S(2)}) collective-permute-start(bf16[1040,128]{1,0:T(8,128)(2,1)S(1)} %shard_map.28.refs_5_), channel_id=1, source_target_pairs={{0,2},{1,5},{2,0},{3,7},{4,6},{5,1},{6,4},{7,3},{8,10},{9,13},{10,... | collective-permute-start | bytes 798728 | tf_op jit(solution)/shard_map/ppermute | solution.py:219
  6.8 0.0 collective-permute-start.2
  6.8 1.6 %collective-permute-start.1 = (bf16[1040,128]{1,0:T(8,128)(2,1)S(1)}, bf16[1040,128]{1,0:T(8,128)(2,1)S(1)}, u32[]{:S(2)}, u32[]{:S(2)}) collective-permute-start(bf16[1040,128]{1,0:T(8,128)(2,1)S(1)} %shard_map.28.refs_5_), channel_id=1, source_target_pairs={{0,4},{1,9},{2,6},{3,11},{4,0},{5,13},{6,2},{7,15},{8,12},{9,5},{1... | collective-permute-start | bytes 798728 | tf_op jit(solution)/shard_map/ppermute | solution.py:219
  8.4 0.0 collective-permute-start
  8.4 4.7 %collective-permute-done.4.refs_4_ = bf16[1040,128]{1,0:T(8,128)(2,1)S(1)} collective-permute-done((bf16[1040,128]{1,0:T(8,128)(2,1)S(1)}, bf16[1040,128]{1,0:T(8,128)(2,1)S(1)}, u32[]{:S(2)}, u32[]{:S(2)}) %collective-permute-start.4) | collective-permute-done | bytes 266272 | tf_op jit(solution)/shard_map/ppermute | solution.py:219
  13.1 0.0 collective-permute-done.3.refs_3_
  13.1 0.0 collective-permute-done.2.refs_2_
  13.1 3.8 %collective-permute-done.1.refs_1_ = bf16[1040,128]{1,0:T(8,128)(2,1)S(1)} collective-permute-done((bf16[1040,128]{1,0:T(8,128)(2,1)S(1)}, bf16[1040,128]{1,0:T(8,128)(2,1)S(1)}, u32[]{:S(2)}, u32[]{:S(2)}) %collective-permute-start.1) | collective-permute-done | bytes 266272 | tf_op jit(solution)/shard_map/ppermute | solution.py:219
  16.9 0.2 collective-permute-done.refs_0_
  17.1 0.5 %shard_map.30 = (f32[1,128]{1,0:T(1,128)S(1)}, f32[2,128]{1,0:T(2,128)S(1)}, f32[2,128]{1,0:T(2,128)S(1)}) custom-call(bf16[1040,128]{1,0:T(8,128)(2,1)S(1)} %collective-permute-done.refs_0_, bf16[1040,128]{1,0:T(8,128)(2,1)S(1)} %collective-permute-done.1.refs_1_, bf16[1040,128]{1,0:T(8,128)(2,1)S(1)} %collective-permute-done.2.refs_2_, ...), custom_call_target="tpu_custom_call" | custom-call | flops 204472320 | bytes 1331200 | tf_op jit(solution)/shard_map/pallas_call | solution.py:236
  17.7 0.7 %collective-permute-start.6 = (f32[2,128]{1,0:T(2,128)S(1)}, f32[2,128]{1,0:T(2,128)S(1)}, u32[]{:S(2)}, u32[]{:S(2)}) collective-permute-start(f32[2,128]{1,0:T(2,128)S(1)} %get-tuple-element.10), channel_id=1, source_target_pairs={{0,2},{1,3},{2,0},{3,1},{4,6},{5,7},{6,4},{7,5},{8,10},{9,11},{10,... | collective-permute-start | bytes 3080 | tf_op jit(solution)/shard_map/ppermute | solution.py:204
  18.4 4.1 %collective-permute-start.5 = (f32[1,128]{1,0:T(1,128)S(1)}, f32[1,128]{1,0:T(1,128)S(1)}, u32[]{:S(2)}, u32[]{:S(2)}) collective-permute-start(f32[1,128]{1,0:T(1,128)S(1)} %get-tuple-element.8), channel_id=1, source_target_pairs={{0,12},{1,13},{2,14},{3,15},{8,0},{9,1},{10,2},{11,3},{4,8},{5,9},... | collective-permute-start | bytes 1544 | tf_op jit(solution)/shard_map/ppermute | solution.py:191
  22.6 0.0 collective-permute-done.6
  22.6 0.1 collective-permute-start.7
  22.6 0.5 %shard_map.29 = f32[1,128]{1,0:T(1,128)S(1)} custom-call(bf16[1040,128]{1,0:T(8,128)(2,1)S(1)} %collective-permute-done.refs_0_, bf16[1040,128]{1,0:T(8,128)(2,1)S(1)} %collective-permute-done.1.refs_1_, bf16[1040,128]{1,0:T(8,128)(2,1)S(1)} %collective-permute-done.2.refs_2_, bf16[1040,128]{1,0:T(8,128)(2,1)S(1)} %collective-permute-done.3.refs_3_, ...), custom_call_target="tpu_custom_call" | custom-call | flops 102236160 | bytes 1064960 | tf_op jit(solution)/shard_map/pallas_call | solution.py:246
  23.2 0.7 %collective-permute-done.5 = f32[1,128]{1,0:T(1,128)S(1)} collective-permute-done((f32[1,128]{1,0:T(1,128)S(1)}, f32[1,128]{1,0:T(1,128)S(1)}, u32[]{:S(2)}, u32[]{:S(2)}) %collective-permute-start.5) | collective-permute-done | bytes 544 | tf_op jit(solution)/shard_map/ppermute | solution.py:191
  23.8 0.0 collective-permute-done.7
  23.9 0.5 %maximum_bitcast_fusion = f32[128]{0:T(128)} fusion(f32[2,128]{1,0:T(2,128)S(1)} %max.13, f32[1,128]{1,0:T(1,128)S(1)} %collective-permute-done.7, f32[1,128]{1,0:T(1,128)S(1)} %shard_map.29, f32[1,128]{1,0:T(1,128)S(1)} %collective-permute-done.5), kind=kLoop, calls=%fused_computation | loop fusion | flops 384 | bytes 2560 | tf_op jit(solution)/shard_map/reshape | solution.py:265
  (2 shorter events, 0.0 us)
Async XLA Ops:
  1.2 11.9 %collective-permute-start.4 = (bf16[1040,128]{1,0:T(8,128)(2,1)S(1)}, bf16[1040,128]{1,0:T(8,128)(2,1)S(1)}, u32[]{:S(2)}, u32[]{:S(2)}) collective-permute-start(bf16[1040,128]{1,0:T(8,128)(2,1)S(1)} %shard_map.28.refs_5_), channel_id=1, source_target_pairs={{0,8},{1,3},{2,10},{3,1},{4,12},{5,7},{6,14},{7,5},{8,4},{9,11},{1... | collective-permute-start | bytes 798728 | tf_op jit(solution)/shard_map/ppermute | solution.py:219
  5.3 7.8 %collective-permute-start.3 = (bf16[1040,128]{1,0:T(8,128)(2,1)S(1)}, bf16[1040,128]{1,0:T(8,128)(2,1)S(1)}, u32[]{:S(2)}, u32[]{:S(2)}) collective-permute-start(bf16[1040,128]{1,0:T(8,128)(2,1)S(1)} %shard_map.28.refs_5_), channel_id=1, source_target_pairs={{0,2},{1,5},{2,0},{3,7},{4,6},{5,1},{6,4},{7,3},{8,10},{9,13},{10,... | collective-permute-start | bytes 798728 | tf_op jit(solution)/shard_map/ppermute | solution.py:219
  6.8 6.3 %collective-permute-start.2 = (bf16[1040,128]{1,0:T(8,128)(2,1)S(1)}, bf16[1040,128]{1,0:T(8,128)(2,1)S(1)}, u32[]{:S(2)}, u32[]{:S(2)}) collective-permute-start(bf16[1040,128]{1,0:T(8,128)(2,1)S(1)} %shard_map.28.refs_5_), channel_id=1, source_target_pairs={{0,1},{1,0},{2,3},{3,2},{4,5},{5,4},{6,7},{7,6},{8,9},{9,8},{10,11... | collective-permute-start | bytes 798728 | tf_op jit(solution)/shard_map/ppermute | solution.py:194
  6.8 10.1 %collective-permute-start.1 = (bf16[1040,128]{1,0:T(8,128)(2,1)S(1)}, bf16[1040,128]{1,0:T(8,128)(2,1)S(1)}, u32[]{:S(2)}, u32[]{:S(2)}) collective-permute-start(bf16[1040,128]{1,0:T(8,128)(2,1)S(1)} %shard_map.28.refs_5_), channel_id=1, source_target_pairs={{0,4},{1,9},{2,6},{3,11},{4,0},{5,13},{6,2},{7,15},{8,12},{9,5},{1... | collective-permute-start | bytes 798728 | tf_op jit(solution)/shard_map/ppermute | solution.py:219
  8.4 8.8 %collective-permute-start = (bf16[1040,128]{1,0:T(8,128)(2,1)S(1)}, bf16[1040,128]{1,0:T(8,128)(2,1)S(1)}, u32[]{:S(2)}, u32[]{:S(2)}) collective-permute-start(bf16[1040,128]{1,0:T(8,128)(2,1)S(1)} %shard_map.28.refs_5_), channel_id=1, source_target_pairs={{0,3},{1,2},{2,1},{3,0},{4,7},{5,6},{6,5},{7,4},{8,11},{9,10},{10,... | collective-permute-start | bytes 798728 | tf_op jit(solution)/shard_map/ppermute | solution.py:194
  17.7 4.9 %collective-permute-start.6 = (f32[2,128]{1,0:T(2,128)S(1)}, f32[2,128]{1,0:T(2,128)S(1)}, u32[]{:S(2)}, u32[]{:S(2)}) collective-permute-start(f32[2,128]{1,0:T(2,128)S(1)} %get-tuple-element.10), channel_id=1, source_target_pairs={{0,2},{1,3},{2,0},{3,1},{4,6},{5,7},{6,4},{7,5},{8,10},{9,11},{10,... | collective-permute-start | bytes 3080 | tf_op jit(solution)/shard_map/ppermute | solution.py:204
  18.4 5.4 %collective-permute-start.5 = (f32[1,128]{1,0:T(1,128)S(1)}, f32[1,128]{1,0:T(1,128)S(1)}, u32[]{:S(2)}, u32[]{:S(2)}) collective-permute-start(f32[1,128]{1,0:T(1,128)S(1)} %get-tuple-element.8), channel_id=1, source_target_pairs={{0,12},{1,13},{2,14},{3,15},{8,0},{9,1},{10,2},{11,3},{4,8},{5,9},... | collective-permute-start | bytes 1544 | tf_op jit(solution)/shard_map/ppermute | solution.py:191
  22.6 1.3 %collective-permute-start.7 = (f32[1,128]{1,0:T(1,128)S(1)}, f32[1,128]{1,0:T(1,128)S(1)}, u32[]{:S(2)}, u32[]{:S(2)}) collective-permute-start(f32[1,128]{1,0:T(1,128)S(1)} %slice.6), channel_id=1, source_target_pairs={{0,1},{1,0},{2,3},{3,2},{4,5},{5,4},{6,7},{7,6},{8,9},{9,8},{10,11... | collective-permute-start | bytes 1544 | tf_op jit(solution)/shard_map/ppermute | solution.py:204

commit v7 on v5

--- a/solution.py
+++ b/solution.py
@@ -26,9 +26,9 @@
         for c in range(CHUNKS)
     ]
     copy_ids = pltpu.make_async_copy(ids_hbm, ids_ref, ids_sem)
-    copy_ids.start()
     for copy in copies:
         copy.start()
+    copy_ids.start()
     copy_ids.wait()
     ids = ids_ref[...].astype(jnp.float32)
     out_ref[pl.ds(width // LANES * rows, ID_ROWS), :] = jnp.broadcast_to(
@@ -110,13 +110,18 @@
     refs[-1][...] = row_maxima(masked_scores(column[:1], column, rows, True)[0])
 
 
-def moved_kernel(*refs, rows, place, last):
+def moved_kernel(*refs, rows, place, turns, last):
     left = [refs[i] for i in place["left"]]
     column = [refs[i] for i in place["column"]]
-    turn_ref, part_ref = refs[-2:]
+    *turn_refs, pass_ref, keep_ref = refs[-2 - max(turns, 1) :]
     masked = masked_scores(left, column, rows, False)
-    for t in range(len(left)):
-        turn_ref[t] = row_maxima(masked[t])
+    odd = lax.rem(lax.axis_index("sub"), 2) == 1
+    for t in range(turns):
+        best = functools.reduce(jnp.maximum, masked[t])
+        if len(left) > 1:
+            other = functools.reduce(jnp.maximum, masked[-1 - t])
+            best = jnp.where(odd, other, best)
+        turn_refs[t][...] = jnp.max(best.T, axis=0, keepdims=True)
     parts = []
     for k in range(len(column)):
         part = functools.reduce(jnp.maximum, [masked[t][k] for t in range(len(left))])
@@ -128,7 +133,8 @@
             jnp.where(here, parts[1], parts[2]),
         )
     for k, part in enumerate(parts):
-        part_ref[pl.ds(k, 1), :] = part
+        ref, row = (keep_ref, k) if k < 2 else (pass_ref, k - 2)
+        ref[pl.ds(row, 1), :] = part
 
 
 def cost(lefts, column):
@@ -186,11 +192,13 @@
         "left": [names.index(("left", t)) for t in range(len(left))],
         "column": [names.index(("column", k)) for k in range(lanes)],
     }
-    turn_best, part = pl.pallas_call(
-        functools.partial(moved_kernel, rows=rows, place=place, last=last),
-        out_shape=[
-            jax.ShapeDtypeStruct((len(left), 1, rows), jnp.float32),
-            jax.ShapeDtypeStruct((lanes, rows), jnp.float32),
+    line = jax.ShapeDtypeStruct((1, rows), jnp.float32)
+    *back, passed, kept = pl.pallas_call(
+        functools.partial(moved_kernel, rows=rows, place=place, turns=len(turns), last=last),
+        out_shape=[line] * max(len(turns), 1)
+        + [
+            jax.ShapeDtypeStruct((max(lanes - 2, 1), rows), jnp.float32),
+            jax.ShapeDtypeStruct((2, rows), jnp.float32),
         ],
         cost_estimate=cost(len(left), column),
         compiler_params=pltpu.CompilerParams(vmem_limit_bytes=VMEM_BYTES),
@@ -202,18 +210,16 @@
         compiler_params=pltpu.CompilerParams(vmem_limit_bytes=VMEM_BYTES),
     )(*blocks)
 
-    odd = lax.axis_index("sub") % 2 == 1
     best = [own_best]
-    for t, step in enumerate(turns):
-        back = jnp.where(odd, turn_best[len(steps) - 1 - t], turn_best[t])
-        best.append(along_dev(back, (-step, -step)))
+    for value, step in zip(back, turns):
+        best.append(along_dev(value, (-step, -step)))
     if last:
-        pair = jnp.maximum(part[:2], by_column(part[2:], 2, 1))
+        pair = jnp.maximum(kept, by_column(passed, 2, 1))
         best.append(by_column(pair[1:], 1, 2))
     else:
-        pair = part[:2]
+        pair = kept
         for flip in range(2, lanes, 2):
-            pair = jnp.maximum(pair, along_sub(part[flip : flip + 2], flip))
+            pair = jnp.maximum(pair, along_sub(passed[flip - 2 : flip], flip))
         best.append(along_sub(pair[1:], 1))
     best.append(pair[:1])
     return functools.reduce(jnp.maximum, best).reshape(rows)

time: 24.6 us -> 24.6 us (level)
  no operation moved by 1% of the time
where the time goes in v7:
time: 24.6 us; the launch traced here: 24.4 us
  starting transfers between devices  11.9 us (48%)
  waiting for transfers between devices  9.64 us (39%)
  Pallas kernels  2.29 us (9%)
  other arithmetic  0.52 us (2%)
    ppermute x3, starting transfers between devices, along_dev(): return lax.ppermute(value, ('dev', 'sub'), pairs)  9.27 us
    ppermute x3, waiting for transfers between devices, along_dev(): return lax.ppermute(value, ('dev', 'sub'), pairs)  6.4 us
    ppermute x3, waiting for transfers between devices, along_sub(): return lax.ppermute(value, 'sub', [(i, i ^ flip) for i in range(lanes)])  3.23 us
    ppermute x3, starting transfers between devices, along_sub(): return lax.ppermute(value, 'sub', [(i, i ^ flip) for i in range(lanes)])  1.5 us
    pallas_call x1, Pallas kernels, pack(): pl.pallas_call(pack_kernel, out_shape=jax.ShapeDtypeStruct((width // LANE...  1.18 us
    ppermute x2, starting transfers between devices, by_column(): return lax.ppermute(value, ('dev', 'sub'), pairs)  1.15 us
    pallas_call x1, Pallas kernels, on_device(): pl.pallas_call(functools.partial(moved_kernel, rows=rows, place=place, tu...  0.55 us
    pallas_call x1, Pallas kernels, on_device(): pl.pallas_call(functools.partial(own_kernel, rows=rows, place=place), out...  0.55 us
  transfers between devices with their start and end apart: 8, of which 5 were waited for; matrix products, arithmetic and copies ran while one was open for 0% of the time, Pallas kernels for 2%

profile of v7, /device:TPU:0, one launch (start us, length us, event | category | flops | bytes accessed | tf_op | source)
XLA Modules:
  0.0 24.4 jit_solution(7149328016720870875)
XLA Ops:
  0.0 1.2 %shard_map.28.refs_5_ = bf16[1040,128]{1,0:T(8,128)(2,1)S(1)} custom-call(f32[128,1024]{1,0:T(8,128)} %embeds_hbm.1, s32[1,128]{1,0:T(1,128)} %bitcast.3), custom_call_target="tpu_custom_call" | custom-call | tf_op jit(solution)/shard_map/pallas_call | solution.py:54
  1.2 4.1 %collective-permute-start.4 = (bf16[1040,128]{1,0:T(8,128)(2,1)S(1)}, bf16[1040,128]{1,0:T(8,128)(2,1)S(1)}, u32[]{:S(2)}, u32[]{:S(2)}) collective-permute-start(bf16[1040,128]{1,0:T(8,128)(2,1)S(1)} %shard_map.28.refs_5_), channel_id=1, source_target_pairs={{0,8},{1,5},{2,10},{3,7},{8,4},{9,13},{10,6},{11,15},{4,12},{5,1},... | collective-permute-start | bytes 798728 | tf_op jit(solution)/shard_map/ppermute | solution.py:164
  5.3 1.5 %collective-permute-start.3 = (bf16[1040,128]{1,0:T(8,128)(2,1)S(1)}, bf16[1040,128]{1,0:T(8,128)(2,1)S(1)}, u32[]{:S(2)}, u32[]{:S(2)}) collective-permute-start(bf16[1040,128]{1,0:T(8,128)(2,1)S(1)} %shard_map.28.refs_5_), channel_id=1, source_target_pairs={{0,2},{1,3},{2,0},{3,1},{4,6},{5,7},{6,4},{7,5},{8,10},{9,11},{10,... | collective-permute-start | bytes 798728 | tf_op jit(solution)/shard_map/ppermute | solution.py:167
  6.8 0.0 collective-permute-start.2
  6.8 1.6 %collective-permute-start.1 = (bf16[1040,128]{1,0:T(8,128)(2,1)S(1)}, bf16[1040,128]{1,0:T(8,128)(2,1)S(1)}, u32[]{:S(2)}, u32[]{:S(2)}) collective-permute-start(bf16[1040,128]{1,0:T(8,128)(2,1)S(1)} %shard_map.28.refs_5_), channel_id=1, source_target_pairs={{0,4},{1,9},{2,6},{3,11},{8,12},{9,5},{10,14},{11,7},{4,0},{5,13},... | collective-permute-start | bytes 798728 | tf_op jit(solution)/shard_map/ppermute | solution.py:164
  8.4 0.0 collective-permute-start
  8.4 5.3 %collective-permute-done.4.refs_4_ = bf16[1040,128]{1,0:T(8,128)(2,1)S(1)} collective-permute-done((bf16[1040,128]{1,0:T(8,128)(2,1)S(1)}, bf16[1040,128]{1,0:T(8,128)(2,1)S(1)}, u32[]{:S(2)}, u32[]{:S(2)}) %collective-permute-start.4) | collective-permute-done | bytes 266272 | tf_op jit(solution)/shard_map/ppermute | solution.py:164
  13.6 0.9 %collective-permute-done.3.refs_3_ = bf16[1040,128]{1,0:T(8,128)(2,1)S(1)} collective-permute-done((bf16[1040,128]{1,0:T(8,128)(2,1)S(1)}, bf16[1040,128]{1,0:T(8,128)(2,1)S(1)}, u32[]{:S(2)}, u32[]{:S(2)}) %collective-permute-start.3) | collective-permute-done | bytes 266272 | tf_op jit(solution)/shard_map/ppermute | solution.py:167
  14.5 2.3 %collective-permute-done.2.refs_2_ = bf16[1040,128]{1,0:T(8,128)(2,1)S(1)} collective-permute-done((bf16[1040,128]{1,0:T(8,128)(2,1)S(1)}, bf16[1040,128]{1,0:T(8,128)(2,1)S(1)}, u32[]{:S(2)}, u32[]{:S(2)}) %collective-permute-start.2) | collective-permute-done | bytes 266272 | tf_op jit(solution)/shard_map/ppermute | solution.py:167
  16.8 0.5 %collective-permute-done.1.refs_1_ = bf16[1040,128]{1,0:T(8,128)(2,1)S(1)} collective-permute-done((bf16[1040,128]{1,0:T(8,128)(2,1)S(1)}, bf16[1040,128]{1,0:T(8,128)(2,1)S(1)}, u32[]{:S(2)}, u32[]{:S(2)}) %collective-permute-start.1) | collective-permute-done | bytes 266272 | tf_op jit(solution)/shard_map/ppermute | solution.py:164
  17.3 0.0 collective-permute-done.refs_0_
  17.3 0.6 %shard_map.30 = (f32[1,128]{1,0:T(1,128)S(1)}, f32[2,128]{1,0:T(2,128)S(1)}, f32[2,128]{1,0:T(2,128)S(1)}) custom-call(bf16[1040,128]{1,0:T(8,128)(2,1)S(1)} %collective-permute-done.refs_0_, bf16[1040,128]{1,0:T(8,128)(2,1)S(1)} %collective-permute-done.1.refs_1_, bf16[1040,128]{1,0:T(8,128)(2,1)S(1)} %collective-permute-done.2.refs_2_, ...), custom_call_target="tpu_custom_call" | custom-call | flops 272629760 | bytes 1597440 | tf_op jit(solution)/shard_map/pallas_call | solution.py:196
  17.9 1.1 %collective-permute-start.6 = (f32[2,128]{1,0:T(2,128)S(1)}, f32[2,128]{1,0:T(2,128)S(1)}, u32[]{:S(2)}, u32[]{:S(2)}) collective-permute-start(f32[2,128]{1,0:T(2,128)S(1)} %get-tuple-element.10), channel_id=1, source_target_pairs={{0,2},{1,3},{2,0},{3,1},{4,6},{5,7},{6,4},{7,5},{8,10},{9,11},{10,... | collective-permute-start | bytes 3080 | tf_op jit(solution)/shard_map/ppermute | solution.py:177
  19.0 3.6 %collective-permute-start.5 = (f32[1,128]{1,0:T(1,128)S(1)}, f32[1,128]{1,0:T(1,128)S(1)}, u32[]{:S(2)}, u32[]{:S(2)}) collective-permute-start(f32[1,128]{1,0:T(1,128)S(1)} %get-tuple-element.8), channel_id=1, source_target_pairs={{0,12},{1,13},{2,14},{3,15},{8,0},{9,1},{10,2},{11,3},{4,8},{5,9},... | collective-permute-start | bytes 1544 | tf_op jit(solution)/shard_map/ppermute | solution.py:164
  22.6 0.0 collective-permute-done.6
  22.6 0.1 collective-permute-start.7
  22.7 0.5 %shard_map.29 = f32[1,128]{1,0:T(1,128)S(1)} custom-call(bf16[1040,128]{1,0:T(8,128)(2,1)S(1)} %collective-permute-done.refs_0_, bf16[1040,128]{1,0:T(8,128)(2,1)S(1)} %collective-permute-done.1.refs_1_, bf16[1040,128]{1,0:T(8,128)(2,1)S(1)} %collective-permute-done.2.refs_2_, bf16[1040,128]{1,0:T(8,128)(2,1)S(1)} %collective-permute-done.3.refs_3_, ...), custom_call_target="tpu_custom_call" | custom-call | flops 136314880 | bytes 1331200 | tf_op jit(solution)/shard_map/pallas_call | solution.py:206
  23.2 0.6 %collective-permute-done.5 = f32[1,128]{1,0:T(1,128)S(1)} collective-permute-done((f32[1,128]{1,0:T(1,128)S(1)}, f32[1,128]{1,0:T(1,128)S(1)}, u32[]{:S(2)}, u32[]{:S(2)}) %collective-permute-start.5) | collective-permute-done | bytes 544 | tf_op jit(solution)/shard_map/ppermute | solution.py:164
  23.9 0.0 collective-permute-done.7
  23.9 0.5 %maximum_bitcast_fusion = f32[128]{0:T(128)} fusion(f32[2,128]{1,0:T(2,128)S(1)} %max.13, f32[1,128]{1,0:T(1,128)S(1)} %collective-permute-done.7, f32[1,128]{1,0:T(1,128)S(1)} %shard_map.29, f32[1,128]{1,0:T(1,128)S(1)} %collective-permute-done.5), kind=kLoop, calls=%fused_computation | loop fusion | flops 384 | bytes 2560 | tf_op jit(solution)/shard_map/reshape | solution.py:225
  (2 shorter events, 0.0 us)
Async XLA Ops:
  1.2 12.4 %collective-permute-start.4 = (bf16[1040,128]{1,0:T(8,128)(2,1)S(1)}, bf16[1040,128]{1,0:T(8,128)(2,1)S(1)}, u32[]{:S(2)}, u32[]{:S(2)}) collective-permute-start(bf16[1040,128]{1,0:T(8,128)(2,1)S(1)} %shard_map.28.refs_5_), channel_id=1, source_target_pairs={{0,8},{1,5},{2,10},{3,7},{8,4},{9,13},{10,6},{11,15},{4,12},{5,1},... | collective-permute-start | bytes 798728 | tf_op jit(solution)/shard_map/ppermute | solution.py:164
  5.3 9.2 %collective-permute-start.3 = (bf16[1040,128]{1,0:T(8,128)(2,1)S(1)}, bf16[1040,128]{1,0:T(8,128)(2,1)S(1)}, u32[]{:S(2)}, u32[]{:S(2)}) collective-permute-start(bf16[1040,128]{1,0:T(8,128)(2,1)S(1)} %shard_map.28.refs_5_), channel_id=1, source_target_pairs={{0,2},{1,3},{2,0},{3,1},{4,6},{5,7},{6,4},{7,5},{8,10},{9,11},{10,... | collective-permute-start | bytes 798728 | tf_op jit(solution)/shard_map/ppermute | solution.py:167
  6.8 10.1 %collective-permute-start.2 = (bf16[1040,128]{1,0:T(8,128)(2,1)S(1)}, bf16[1040,128]{1,0:T(8,128)(2,1)S(1)}, u32[]{:S(2)}, u32[]{:S(2)}) collective-permute-start(bf16[1040,128]{1,0:T(8,128)(2,1)S(1)} %shard_map.28.refs_5_), channel_id=1, source_target_pairs={{0,3},{1,2},{2,1},{3,0},{4,7},{5,6},{6,5},{7,4},{8,11},{9,10},{10,... | collective-permute-start | bytes 798728 | tf_op jit(solution)/shard_map/ppermute | solution.py:167
  6.8 10.6 %collective-permute-start.1 = (bf16[1040,128]{1,0:T(8,128)(2,1)S(1)}, bf16[1040,128]{1,0:T(8,128)(2,1)S(1)}, u32[]{:S(2)}, u32[]{:S(2)}) collective-permute-start(bf16[1040,128]{1,0:T(8,128)(2,1)S(1)} %shard_map.28.refs_5_), channel_id=1, source_target_pairs={{0,4},{1,9},{2,6},{3,11},{8,12},{9,5},{10,14},{11,7},{4,0},{5,13},... | collective-permute-start | bytes 798728 | tf_op jit(solution)/shard_map/ppermute | solution.py:164
  8.4 9.0 %collective-permute-start = (bf16[1040,128]{1,0:T(8,128)(2,1)S(1)}, bf16[1040,128]{1,0:T(8,128)(2,1)S(1)}, u32[]{:S(2)}, u32[]{:S(2)}) collective-permute-start(bf16[1040,128]{1,0:T(8,128)(2,1)S(1)} %shard_map.28.refs_5_), channel_id=1, source_target_pairs={{0,1},{1,0},{2,3},{3,2},{4,5},{5,4},{6,7},{7,6},{8,9},{9,8},{10,11... | collective-permute-start | bytes 798728 | tf_op jit(solution)/shard_map/ppermute | solution.py:167
  17.9 4.7 %collective-permute-start.6 = (f32[2,128]{1,0:T(2,128)S(1)}, f32[2,128]{1,0:T(2,128)S(1)}, u32[]{:S(2)}, u32[]{:S(2)}) collective-permute-start(f32[2,128]{1,0:T(2,128)S(1)} %get-tuple-element.10), channel_id=1, source_target_pairs={{0,2},{1,3},{2,0},{3,1},{4,6},{5,7},{6,4},{7,5},{8,10},{9,11},{10,... | collective-permute-start | bytes 3080 | tf_op jit(solution)/shard_map/ppermute | solution.py:177
  19.0 4.9 %collective-permute-start.5 = (f32[1,128]{1,0:T(1,128)S(1)}, f32[1,128]{1,0:T(1,128)S(1)}, u32[]{:S(2)}, u32[]{:S(2)}) collective-permute-start(f32[1,128]{1,0:T(1,128)S(1)} %get-tuple-element.8), channel_id=1, source_target_pairs={{0,12},{1,13},{2,14},{3,15},{8,0},{9,1},{10,2},{11,3},{4,8},{5,9},... | collective-permute-start | bytes 1544 | tf_op jit(solution)/shard_map/ppermute | solution.py:164
  22.6 1.3 %collective-permute-start.7 = (f32[1,128]{1,0:T(1,128)S(1)}, f32[1,128]{1,0:T(1,128)S(1)}, u32[]{:S(2)}, u32[]{:S(2)}) collective-permute-start(f32[1,128]{1,0:T(1,128)S(1)} %slice.6), channel_id=1, source_target_pairs={{0,1},{1,0},{2,3},{3,2},{4,5},{5,4},{6,7},{7,6},{8,9},{9,8},{10,11... | collective-permute-start | bytes 1544 | tf_op jit(solution)/shard_map/ppermute | solution.py:177
